TPU v7x, 128 devices: a whole 4x4x4 slice. The times are simulated.
128 devices in a mesh: row: 16 (over z, x), col: 8 (over y, core).
Axes of the slice: x: 4, y: 4, z: 4, core: 2. Of those that a mesh axis runs over, the one named last changes fastest.
Arguments:
- features: bfloat16 [262144, 512], P(('row', 'col')), may hold values from -12 to 12
- targets: bfloat16 [262144, 128], P(('row', 'col')), may hold values from -6 to 6
- primary: float32 [262144, 128], P(('row', 'col')), may hold values from -1.5 to 1.5
- auxiliary: float32 [262144, 128], P(('row', 'col')), may hold values from -1.5 to 1.5
- factors: bfloat16 [2, 2048, 512], replicated, may hold values from -0.125 to 0.125
- spectrum: float32 [2, 512], replicated, may hold values from 1 to 100
- indices: int32 [2, 2048], replicated, may hold values from 0 to 262143, as said below
Outputs:
- primary_out: float32 [262144, 128], P(('row', 'col'))
- auxiliary_out: float32 [262144, 128], P(('row', 'col'))
Inputs may be any that keep to these rules, and one draw needn't show every extreme that they name: For each step the 2048 indices are distinct, and entries k * 16 to (k + 1) * 16 - 1 lie among rows k * 2048 to (k + 1) * 2048 - 1, in no particular order; rows k * 2048 and (k + 1) * 2048 - 1 are always among them.
All inputs are finite; a program needn't handle non-finite values.
Results may differ from a plain program's by a relative error of at most 0.0033.
Values may be sent and summed in bfloat16 or wider, within the bound.
No kernel may reach another device: no remote copies, remote signals or barrier semaphores. Data moves between devices by JAX's collectives and lax.ppermute only.
A program may use at most 64 MiB of HBM per device.

v0:
```python
import jax
import jax.numpy as jnp
from jax import lax
from jax.sharding import PartitionSpec as P

BLOCK = 2048
STEPS = 2


ridge_coef = 0.5
shift_rho = 1.0
step_eta = 0.5
beta_coef = 0.8
gamma_coef = 0.3
alpha_coef = 0.6


def kernel_rows(block, features, row_norms, blend_bf):
    block_norms = jnp.sum(jnp.square(block.astype(jnp.float32)), axis=1)
    inner = lax.dot_general(
        block, features, (((1,), (1,)), ((), ())), preferred_element_type=jnp.float32
    )
    dist = block_norms[:, None] + row_norms[None, :] - 2.0 * inner
    kernel = jnp.exp(-dist / (2.0 * block.shape[1])).astype(jnp.bfloat16)
    return jnp.dot(kernel, blend_bf, preferred_element_type=jnp.float32)


def kernel_term(block, features, row_norms, blend_bf):
    count = block.shape[0]
    pieces = block.reshape(count // 512, 512, block.shape[1])

    def single(piece):
        return kernel_rows(piece, features, row_norms, blend_bf)

    result = lax.map(single, pieces)
    return result.reshape(count, blend_bf.shape[1])


def apply_inverse(gradient, factor, spectrum_row, reducer):
    coef = 1.0 / (spectrum_row + shift_rho) - 1.0 / shift_rho
    projected = reducer(jnp.dot(factor.T, gradient, precision=lax.Precision.HIGHEST))
    return gradient / shift_rho + jnp.dot(
        factor, coef[:, None] * projected, precision=lax.Precision.HIGHEST
    )


def on_device(features, targets, primary, auxiliary, factors, spectrum, indices):
    rows_here = features.shape[0]
    n_devices = lax.axis_size("row") * lax.axis_size("col")
    per_device = BLOCK // n_devices
    position = lax.axis_index("row") * lax.axis_size("col") + lax.axis_index("col")
    first = position * per_device
    row_norms = jnp.sum(jnp.square(features.astype(jnp.float32)), axis=1)
    blend = alpha_coef * auxiliary + (1.0 - alpha_coef) * primary

    def reduce_factor(partial_value):
        return lax.psum(partial_value, ("row", "col"))

    for step in range(STEPS):
        own_rows = (
            lax.dynamic_slice_in_dim(indices[step], first, per_device, 0) - position * rows_here
        )
        own_feat = features[own_rows]
        block = lax.all_gather(own_feat, ("row", "col"), axis=0, tiled=True)
        blend_bf = blend.astype(jnp.bfloat16)
        own_extra = ridge_coef * blend[own_rows] - targets[own_rows].astype(jnp.float32)
        factor_all = factors[step]
        gradient = (
            lax.psum_scatter(
                kernel_term(block, features, row_norms, blend_bf),
                ("row", "col"),
                scatter_dimension=0,
                tiled=True,
            )
            + own_extra
        )
        factor_mine = lax.dynamic_slice_in_dim(factor_all, first, per_device, 0).astype(jnp.float32)
        direction = apply_inverse(gradient, factor_mine, spectrum[step], reduce_factor)
        primary = blend.at[own_rows].add(-step_eta * direction)
        auxiliary = beta_coef * auxiliary + (1.0 - beta_coef) * blend
        auxiliary = auxiliary.at[own_rows].add(-gamma_coef * direction)
        blend = alpha_coef * auxiliary + (1.0 - alpha_coef) * primary
    return (primary, auxiliary)


def solution(mesh):
    return jax.shard_map(
        on_device,
        mesh=mesh,
        in_specs=(
            P(("row", "col"), None),
            P(("row", "col"), None),
            P(("row", "col"), None),
            P(("row", "col"), None),
            P(),
            P(),
            P(),
        ),
        out_specs=(P(("row", "col"), None), P(("row", "col"), None)),
        check_vma=False,
    )
```

profile of v0, /device:TPU:1, one launch (start us, length us, event | category | flops | bytes accessed | tf_op | source)
XLA Modules:
  0.0 1754.1 jit_solution(7467424007940632471)
XLA Ops:
  7.2 0.8 fusion.57
  8.0 0.1 fusion.52
  8.1 3.1 gather_fusion
  11.3 2.9 multiply_add_fusion.2
  14.3 0.5 multiply_reduce_fusion.2
  14.8 66.0 %all-gather.5.cloned.1.call-done = bf16[2048,512]{1,0:T(8,128)(2,1)} async-done(((bf16[16,512]{1,0:T(8,128)(2,1)}), bf16[2048,512]{1,0:T(8,128)(2,1)}) %all-gather.5.cloned.1.call-update) | async-done | bytes 2097168 | tf_op jit(solution)/shard_map/all_gather | solution.py:64
  80.7 0.1 broadcast.140.clone
  80.8 20.0 %while.20 = (s32[]{:T(128)}, f32[4,512,128]{2,1,0:T(8,128)S(1)}, bf16[4,512,512]{2,1,0:T(8,128)(2,1)}, f32[2048]{0:T(1024)S(1)}, bf16[2048,512]{1,0:T(8,128)(2,1)}, /*index=5*/bf16[2048,128]{1,0:T(8,128)(2,1)S(1)}, s32[]{:T(128)}) while((s32[]{:T(128)}, f32[4,512,128]{2,1,0:T(8,128)S(1)}, bf16[4,512,512]{2,1,0:T(8,128)(2,1)}, ...), condition=%wide.region_3.4_spmd, body=%wide.region_1.3_spmd.sunk | while | flops 1349254656 | bytes 3945553 | solution.py:35
  80.8 1.2 multiply_reduce_fusion.5
  82.0 3.8 fusion.73
  85.8 1.2 multiply_reduce_fusion.5
  87.0 3.7 fusion.73
  90.8 1.2 multiply_reduce_fusion.5
  92.0 3.8 fusion.73
  95.8 1.2 multiply_reduce_fusion.5
  97.0 3.7 fusion.73
  100.8 1.0 copy-done.3
  101.8 0.6 gather_fusion.1
  102.4 0.6 gather_fusion.2
  103.0 4.5 fusion.56
  107.5 623.7 %reduce-scatter.3.cloned.1.call-done = f32[16,128]{1,0:T(8,128)} async-done(((f32[2048,128]{1,0:T(8,128)}), f32[16,128]{1,0:T(8,128)}) %reduce-scatter.3.cloned.1.call-update) | async-done | bytes 8208 | tf_op jit(solution)/shard_map/reduce_scatter | solution.py:69
  731.1 1.7 fusion.26
  733.0 0.1 fusion.53
  733.0 3.0 gather_fusion.3
  736.2 143.0 %all-reduce.3.cloned.1.call-done = f32[512,128]{1,0:T(8,128)} async-done(((f32[512,128]{1,0:T(8,128)}), f32[512,128]{1,0:T(8,128)}) %all-reduce.3.cloned.1.call-update) | async-done | bytes 262160 | tf_op jit(solution)/shard_map/psum | solution.py:57
  879.2 1.2 convolution_add_fusion.1
  880.5 1.1 scatter_custom_fusion.1
  881.5 2.8 scatter_custom_fusion
  884.3 2.5 multiply_add_fusion
  886.9 59.0 %all-gather.7.cloned.1.call-done = bf16[2048,512]{1,0:T(8,128)(2,1)} async-done(((bf16[16,512]{1,0:T(8,128)(2,1)}), bf16[2048,512]{1,0:T(8,128)(2,1)}) %all-gather.7.cloned.1.call-update) | async-done | bytes 2097168 | tf_op jit(solution)/shard_map/all_gather | solution.py:64
  945.9 20.0 %while.21 = (s32[]{:T(128)}, f32[4,512,128]{2,1,0:T(8,128)S(1)}, bf16[4,512,512]{2,1,0:T(8,128)(2,1)}, f32[2048]{0:T(1024)S(1)}, bf16[2048,512]{1,0:T(8,128)(2,1)}, /*index=5*/bf16[2048,128]{1,0:T(8,128)(2,1)S(1)}, s32[]{:T(128)}) while((s32[]{:T(128)}, f32[4,512,128]{2,1,0:T(8,128)S(1)}, bf16[4,512,512]{2,1,0:T(8,128)(2,1)}, ...), condition=%wide.region_10.11_spmd, body=%wide.region_8.10_spmd.sunk | while | flops 1349254656 | bytes 3945553 | solution.py:35
  945.9 1.2 multiply_reduce_fusion.6
  947.1 3.7 fusion.77
  950.9 1.2 multiply_reduce_fusion.6
  952.1 3.8 fusion.77
  955.9 1.2 multiply_reduce_fusion.6
  957.1 3.7 fusion.77
  960.9 1.2 multiply_reduce_fusion.6
  962.1 3.8 fusion.77
  965.9 1.0 copy-done.2
  966.9 0.6 gather_fusion.5
  967.5 0.6 gather_fusion.4
  968.1 626.4 %reduce-scatter.5.cloned.1.call-done = f32[16,128]{1,0:T(8,128)} async-done(((f32[2048,128]{1,0:T(8,128)}), f32[16,128]{1,0:T(8,128)}) %reduce-scatter.5.cloned.1.call-update) | async-done | bytes 8208 | tf_op jit(solution)/shard_map/reduce_scatter | solution.py:69
  1594.5 1.7 fusion.23
  1596.3 145.5 %all-reduce.5.cloned.1.call-done = f32[512,128]{1,0:T(8,128)} async-done(((f32[512,128]{1,0:T(8,128)}), f32[512,128]{1,0:T(8,128)}) %all-reduce.5.cloned.1.call-update) | async-done | bytes 262160 | tf_op jit(solution)/shard_map/psum | solution.py:57
  1741.7 1.2 convolution_add_fusion
  1743.0 1.1 scatter_custom_fusion.2
  1744.0 3.2 scatter_custom_fusion.3
  (28 shorter events, 0.6 us)
Async XLA Ops:
  7.2 95.2 %copy-start = (bf16[2048,128]{1,0:T(8,128)(2,1)S(1)}, bf16[2048,128]{1,0:T(8,128)(2,1)}, u32[]{:S(2)}) copy-start(bf16[2048,128]{1,0:T(8,128)(2,1)} %param.12) | copy-start | bytes 1572868
  7.2 73.6 %all-gather.5.cloned.1.call-start = ((), (), s32[]{:S(2)}) async-start(), calls=%async_computation.6 | async-start | bytes 2113536 | tf_op jit(solution)/shard_map/all_gather | solution.py:64
  11.2 719.9 %reduce-scatter.3.cloned.1.call-start = ((), (), s32[]{:S(2)}) async-start(), calls=%async_computation.2 | async-start | bytes 1056768 | tf_op jit(solution)/shard_map/reduce_scatter | solution.py:69
  11.3 3.0 copy-start.4
  100.8 1.0 copy-start.3
  101.8 777.4 %all-reduce.3.cloned.1.call-start = ((), (), s32[]{:S(2)}) async-start(), calls=%async_computation.3 | async-start | bytes 524288 | tf_op jit(solution)/shard_map/psum | solution.py:57
  103.0 633.2 %copy-start.5 = (f32[2,512]{1,0:T(2,128)S(1)}, f32[2,512]{1,0:T(2,128)}, u32[]{:S(2)}) copy-start(f32[2,512]{1,0:T(2,128)} %param.16) | copy-start | bytes 12292
  732.9 212.9 %all-gather.7.cloned.1.call-start = ((), (), s32[]{:S(2)}) async-start(), calls=%async_computation.7 | async-start | bytes 2113536 | tf_op jit(solution)/shard_map/all_gather | solution.py:64
  736.1 858.4 %reduce-scatter.5.cloned.1.call-start = ((), (), s32[]{:S(2)}) async-start(), calls=%async_computation.4 | async-start | bytes 1056768 | tf_op jit(solution)/shard_map/reduce_scatter | solution.py:69
  965.9 1.0 copy-start.2
  966.9 774.8 %all-reduce.5.cloned.1.call-start = ((), (), s32[]{:S(2)}) async-start(), calls=%async_computation.5 | async-start | bytes 524288 | tf_op jit(solution)/shard_map/psum | solution.py:57
  1744.0 3.2 copy-start.1
Sparse Core Ops, SparseCore 0:
  11.7 68.9 all-gather.4
  101.9 629.1 reduce-scatter.2
  737.2 141.9 all-reduce.2
  882.7 63.1 all-gather.6
  967.0 627.4 reduce-scatter.4
  1599.7 142.0 all-reduce.4
where the time goes:
time: 1760 us; the launch traced here: 1750 us
  waiting for transfers between devices  1660 us (94%)
  matrix products  35.9 us (2%)
  other arithmetic  24 us (1%)
    reduce_scatter x2, waiting for transfers between devices, on_device(): lax.psum_scatter(kernel_term(block, features, row_norms, blend_bf), ('row...  1250 us
    psum x2, waiting for transfers between devices, reduce_factor(): return lax.psum(partial_value, ('row', 'col'))  288 us
    all_gather x2, waiting for transfers between devices, on_device(): block = lax.all_gather(own_feat, ('row', 'col'), axis=0, tiled=True)  125 us
  transfers between devices with their start and end apart: 6, of which 6 were waited for; matrix products, arithmetic and copies ran while one was open for 1% of the time, Pallas kernels for 0%

commit v1 on v0

v1 whole, which is shorter than its diff:
```python
import functools

import jax
import jax.numpy as jnp
from jax import lax
from jax.experimental import pallas as pl
from jax.experimental.pallas import tpu as pltpu
from jax.sharding import Mesh, PartitionSpec as P

STEPS = 2
CHIPS = 64
OWN = 16
ROWS = 2048
D = 512
OUT = 128
LOG2E = 1.4426950408889634
MIB = 1024 * 1024
ALL = ("row", "y", "core")
SAME_CORE = ("row", "y")
TILE_CHIPS = 16
CHUNK = 512
GROUP = 16

ridge_coef = 0.5
shift_rho = 1.0
step_eta = 0.5
beta_coef = 0.8
gamma_coef = 0.3
alpha_coef = 0.6

MOVE = alpha_coef * gamma_coef + (1.0 - alpha_coef) * step_eta
AUX_MOVE = beta_coef * gamma_coef + (1.0 - beta_coef) * MOVE


def chip_index():
    return lax.axis_index("row") * lax.axis_size("y") + lax.axis_index("y")


def nt(a, b):
    return lax.dot_general(a, b, (((1,), (1,)), ((), ())), preferred_element_type=jnp.float32)


def blends(aux, pri):
    blend0 = alpha_coef * aux + (1.0 - alpha_coef) * pri
    aux1 = beta_coef * aux + (1.0 - beta_coef) * blend0
    blend1 = alpha_coef * aux1 + (1.0 - alpha_coef) * blend0
    return blend0, aux1, blend1


def own_row(idx, step, i):
    position = chip_index() * 2 + lax.axis_index("core")
    return idx[step, position * OWN + i] - position * ROWS


def pick_kernel(idx, feat, send, near, rows_ref, sem, send_sem):
    copies = []
    which = lax.broadcasted_iota(jnp.int32, (STEPS * OWN, 1), 0)
    column = jnp.zeros((STEPS * OWN, 1), jnp.int32)
    for at in range(STEPS * OWN):
        row = own_row(idx, at // OWN, at % OWN)
        inside = lax.bitwise_and(row, GROUP - 1)
        first = pl.multiple_of(row - inside, GROUP)
        copies.append(
            pltpu.make_async_copy(
                feat.at[pl.ds(first, GROUP), :], near.at[pl.ds(at * GROUP, GROUP), :], sem.at[at]
            )
        )
        copies[-1].start()
        column = jnp.where(which == at, at * GROUP + inside, column)
    chosen = lax.broadcasted_iota(jnp.int32, (STEPS * OWN, STEPS * OWN * GROUP), 1) == column
    chosen = chosen.astype(jnp.float32).astype(jnp.bfloat16)
    for copy in copies:
        copy.wait()
    rows = jnp.dot(chosen, near[...], preferred_element_type=jnp.float32)
    rows_ref[...] = rows.astype(jnp.bfloat16)
    copies = [
        pltpu.make_async_copy(rows_ref, send.at[chip], send_sem.at[chip]) for chip in range(CHIPS)
    ]
    for copy in copies:
        copy.start()
    for copy in copies:
        copy.wait()


def pick(indices, features):
    return pl.pallas_call(
        pick_kernel,
        out_shape=jax.ShapeDtypeStruct((CHIPS, STEPS * OWN, D), jnp.bfloat16),
        in_specs=[pl.BlockSpec(memory_space=pltpu.SMEM), pl.BlockSpec(memory_space=pl.ANY)],
        out_specs=pl.BlockSpec(memory_space=pl.ANY),
        scratch_shapes=[
            pltpu.VMEM((STEPS * OWN * GROUP, D), jnp.bfloat16),
            pltpu.VMEM((STEPS * OWN, D), jnp.bfloat16),
            pltpu.SemaphoreType.DMA((STEPS * OWN,)),
            pltpu.SemaphoreType.DMA((CHIPS,)),
        ],
        compiler_params=pltpu.CompilerParams(vmem_limit_bytes=58 * MIB),
        name="pick",
    )(indices, features)


def prepare_kernel(idx, tgt, pri, aux, blend_bf, extra, pri_base, aux_base, rows_base):
    blend0, aux1, blend1 = blends(aux[...], pri[...])
    blend_bf[0] = blend0.astype(jnp.bfloat16)
    blend_bf[1] = blend1.astype(jnp.bfloat16)
    pri_base[...] = blend1
    aux_base[...] = beta_coef * aux1 + (1.0 - beta_coef) * blend1
    which = lax.broadcasted_iota(jnp.int32, (STEPS * OWN, 1), 0)
    column = jnp.zeros((STEPS * OWN, 1), jnp.int32)
    for at in range(STEPS * OWN):
        row = own_row(idx, at // OWN, at % OWN)
        column = jnp.where(which == at, row, column)
        here, aux1, here1 = blends(aux[pl.ds(row, 1), :], pri[pl.ds(row, 1), :])
        extra[pl.ds(at, 1), :] = ridge_coef * (here1 if at >= OWN else here)
        rows_base[0, pl.ds(at, 1), :] = here1
        rows_base[1, pl.ds(at, 1), :] = beta_coef * aux1 + (1.0 - beta_coef) * here1
    chosen = lax.broadcasted_iota(jnp.int32, (STEPS * OWN, ROWS), 1) == column
    chosen = chosen.astype(jnp.float32).astype(jnp.bfloat16)
    extra[...] -= jnp.dot(chosen, tgt[...], preferred_element_type=jnp.float32)


def prepare(indices, targets, primary, auxiliary):
    vmem = pl.BlockSpec(memory_space=pltpu.VMEM)
    return pl.pallas_call(
        prepare_kernel,
        out_shape=(
            jax.ShapeDtypeStruct((STEPS, ROWS, OUT), jnp.bfloat16),
            jax.ShapeDtypeStruct((STEPS * OWN, OUT), jnp.float32),
            jax.ShapeDtypeStruct((ROWS, OUT), jnp.float32),
            jax.ShapeDtypeStruct((ROWS, OUT), jnp.float32),
            jax.ShapeDtypeStruct((2, STEPS * OWN, OUT), jnp.float32),
        ),
        in_specs=[pl.BlockSpec(memory_space=pltpu.SMEM)] + [vmem] * 3,
        out_specs=(vmem,) * 5,
        compiler_params=pltpu.CompilerParams(vmem_limit_bytes=16 * MIB),
        name="prepare",
    )(indices, targets, primary, auxiliary)


SCALE = LOG2E / (2.0 * D)


def row_norms(block):
    wide = block.astype(jnp.float32)
    return jnp.sum(wide * wide, axis=1, keepdims=True) * SCALE


def kernel_values(block, block_norms, feat, feat_norms):
    return jnp.exp2(nt(block, feat) * (2.0 * SCALE) - (block_norms + feat_norms))


def norm_row(feat, scale=SCALE):
    wide = feat.astype(jnp.float32)
    wide = wide * wide
    lanes = wide[:, :128]
    for at in range(128, D, 128):
        lanes += wide[:, at:at + 128]
    return jnp.sum(jnp.transpose(lanes), axis=0, keepdims=True) * scale


def product_kernel(block_ref, feat0, feat1, blend0, blend1, out, feat_ref, norms_ref, sems):
    opening = jnp.logical_and(pl.program_id(0) == 0, pl.program_id(1) == 0)
    parts = [(which, at) for which in range(2) for at in range(0, ROWS, CHUNK)]

    def load(which, at):
        return pltpu.make_async_copy(
            (feat0, feat1)[which].at[pl.ds(at, CHUNK), :],
            feat_ref.at[which, pl.ds(at, CHUNK), :],
            sems.at[which, at // CHUNK],
        )

    @pl.when(opening)
    def _():
        for part in parts:
            load(*part).start()
        for part in parts:
            load(*part).wait()
            which, at = part
            norms_ref[which:which + 1, pl.ds(at, CHUNK)] = norm_row(feat_ref[which, pl.ds(at, CHUNK), :])

    block = block_ref[...].reshape(TILE_CHIPS * OWN, D)
    norms = row_norms(block)
    total = jnp.zeros((TILE_CHIPS * OWN, OUT), jnp.float32)
    for which, at in parts:
        part = pl.ds(at, CHUNK)
        kernel = kernel_values(block, norms, feat_ref[which, part, :], norms_ref[which:which + 1, part])
        total += jnp.dot(
            kernel.astype(jnp.bfloat16), (blend0, blend1)[which][0, part, :],
            preferred_element_type=jnp.float32,
        )
    out[...] = total.reshape(out.shape)


def products(block, features, blend_bf):
    tiles = CHIPS // TILE_CHIPS
    blend_spec = pl.BlockSpec((1, ROWS, OUT), lambda s, i: (s, 0, 0))
    return pl.pallas_call(
        product_kernel,
        grid=(STEPS, tiles),
        out_shape=jax.ShapeDtypeStruct((CHIPS, STEPS, OWN, OUT), jnp.float32),
        in_specs=[pl.BlockSpec((TILE_CHIPS, 1, OWN, D), lambda s, i: (i, s, 0, 0))]
        + [pl.BlockSpec(memory_space=pl.ANY)] * 2
        + [blend_spec] * 2,
        out_specs=pl.BlockSpec((TILE_CHIPS, 1, OWN, OUT), lambda s, i: (i, s, 0, 0)),
        scratch_shapes=[
            pltpu.VMEM((2, ROWS, D), jnp.bfloat16),
            pltpu.VMEM((2, ROWS), jnp.float32),
            pltpu.SemaphoreType.DMA((2, ROWS // CHUNK)),
        ],
        compiler_params=pltpu.CompilerParams(vmem_limit_bytes=56 * MIB),
        cost_estimate=pl.CostEstimate(
            flops=2 * 2048 * 4096 * 640, bytes_accessed=9 * MIB, transcendentals=2048 * 4096
        ),
        name="products",
    )(block, *features, *blend_bf)


def cross_kernel(idx_ref, own1, other1, own0, other0, out, token):
    token[...] = jnp.zeros_like(token)
    half = pl.program_id(0)
    tile = pl.program_id(1)
    size = TILE_CHIPS * OWN
    block = jnp.where(half == 0, own1[...], other1[...]).reshape(size, D)
    norms = row_norms(block)
    for which, feat_ref in enumerate((own0, other0)):
        for at in range(0, CHIPS, TILE_CHIPS):
            feat = feat_ref[at:at + TILE_CHIPS, 0].reshape(size, D)
            kernel = kernel_values(block, norms, feat, norm_row(feat))
            left = idx_ref[pl.ds(half, 1), 1, pl.ds(tile, 1), :].reshape(1, size)
            right = idx_ref[which, 0, at // TILE_CHIPS].reshape(1, size)
            left = jnp.transpose(jnp.broadcast_to(left, (size, size)))
            kernel = kernel.astype(jnp.bfloat16).astype(jnp.float32)
            kernel = kernel + jnp.where(left == right, ridge_coef, 0.0)
            start = which * CHIPS * OWN + at * OWN
            out[0, :, :, start:start + size] = kernel.astype(jnp.bfloat16).reshape(TILE_CHIPS, OWN, size)


def cross(own, other, idx):
    tiles = CHIPS // TILE_CHIPS
    tile_spec = pl.BlockSpec((TILE_CHIPS, 1, OWN, D), lambda h, i: (i, 1, 0, 0))
    whole = pl.BlockSpec((CHIPS, 1, OWN, D), lambda h, i: (0, 0, 0, 0))
    return pl.pallas_call(
        cross_kernel,
        grid=(2, tiles),
        out_shape=(
            jax.ShapeDtypeStruct((2, CHIPS, OWN, ROWS), jnp.bfloat16),
            jax.ShapeDtypeStruct((8, 128), jnp.float32),
        ),
        in_specs=[
            pl.BlockSpec((2, STEPS, tiles, TILE_CHIPS * OWN), lambda h, i: (0, 0, 0, 0)),
            tile_spec, tile_spec, whole, whole,
        ],
        out_specs=(
            pl.BlockSpec((1, TILE_CHIPS, OWN, ROWS), lambda h, i: (h, i, 0, 0)),
            pl.BlockSpec((8, 128), lambda h, i: (0, 0)),
        ),
        compiler_params=pltpu.CompilerParams(vmem_limit_bytes=16 * MIB),
        cost_estimate=pl.CostEstimate(
            flops=2 * 2048 * 2048 * 512, bytes_accessed=12 * MIB, transcendentals=2048 * 2048
        ),
        name="cross",
    )(idx, own, other, own, other)


def collect_kernel(received, extra, after, own_grad, send):
    total = jnp.sum(received[...], axis=0) + extra[...]
    own_grad[...] = total
    send[...] = jnp.broadcast_to(total.astype(jnp.bfloat16)[None], send.shape)


def collect(received, extra, after):
    vmem = pl.BlockSpec(memory_space=pltpu.VMEM)
    return pl.pallas_call(
        collect_kernel,
        out_shape=(
            jax.ShapeDtypeStruct((STEPS * OWN, OUT), jnp.float32),
            jax.ShapeDtypeStruct((CHIPS, STEPS * OWN, OUT), jnp.bfloat16),
        ),
        in_specs=[vmem, vmem, pl.BlockSpec(memory_space=pl.ANY)],
        out_specs=(vmem, vmem),
        compiler_params=pltpu.CompilerParams(vmem_limit_bytes=8 * MIB),
        name="collect",
    )(received, extra, after)


def split(x):
    high = x.astype(jnp.bfloat16)
    return high, (x - high.astype(jnp.float32)).astype(jnp.bfloat16)


def split_nt(x, y):
    high, low = split(x)
    both = nt(jnp.concatenate([high, low], axis=0), y)
    return both[: x.shape[0]] + both[x.shape[0]:]


def finish_kernel(
    idx, grads_own, grads_other, own_grad, factors, spectrum, cross_ref, rows_base, pri_in, aux_in,
    pri_out, aux_out, rows, sems,
):
    chip = chip_index()
    core = lax.axis_index("core")
    count = CHIPS * OWN
    coef = 1.0 / (spectrum[...] + shift_rho) - 1.0 / shift_rho

    def factor(step, half):
        return factors[step, :, lax.bitwise_xor(core, half)].reshape(count, D)

    def gradient(step, half):
        grads = grads_other if half else grads_own
        wide = grads[:, step * OWN:(step + 1) * OWN, :].reshape(count, OUT)
        return jnp.transpose(wide.astype(jnp.float32))

    grad0 = [gradient(0, half) for half in range(2)]
    factor0 = [factor(0, half) for half in range(2)]
    projected = jnp.zeros((OUT, D), jnp.float32)
    for half in range(2):
        projected += jnp.dot(
            grad0[half].astype(jnp.bfloat16), factor0[half], preferred_element_type=jnp.float32
        )
    scaled0 = projected * coef[0:1]
    moves = []
    for half in range(2):
        direction = grad0[half] / shift_rho + split_nt(scaled0, factor0[half])
        moves.append((-MOVE * direction).astype(jnp.bfloat16))
    projected = jnp.zeros((OUT, D), jnp.float32)
    for half in range(2):
        grad1 = gradient(1, half)
        for other in range(2):
            part = cross_ref[half, :, :, other * count:(other + 1) * count].reshape(count, count)
            grad1 += nt(moves[other], part)
        both = jnp.dot(
            jnp.concatenate(split(grad1), axis=0), factor(1, half), preferred_element_type=jnp.float32
        )
        projected += both[:OUT] + both[OUT:]
    scaled1 = projected * coef[1:2]

    own_cross = cross_ref[0, chip]
    own0 = own_grad[0:OWN, :]
    own1 = own_grad[OWN:2 * OWN, :]
    for other in range(2):
        own1 += nt(own_cross[:, other * count:(other + 1) * count], moves[other])

    def own_direction(step, grad, scaled):
        high, low = split(scaled)
        mine = factors[step, chip, core]
        return grad / shift_rho + nt(mine, high) + nt(mine, low)

    direction0 = own_direction(0, own0, scaled0)
    direction1 = own_direction(1, own1, scaled1)

    which = lax.broadcasted_iota(jnp.int32, (OWN, 1), 0)
    lanes = lax.broadcasted_iota(jnp.int32, (1, OWN), 1)
    first = jnp.zeros((1, OWN), jnp.int32)
    second = jnp.zeros((OWN, 1), jnp.int32)
    for i in range(OWN):
        first = jnp.where(lanes == i, own_row(idx, 0, i), first)
        second = jnp.where(which == i, own_row(idx, 1, i), second)
    same = first == second
    shared = jnp.zeros((OWN, OUT), jnp.float32)
    for i in range(OWN):
        shared += jnp.where(same[:, i:i + 1], direction0[i:i + 1, :], 0.0)
    for out, moved0, moved1 in ((0, MOVE, step_eta), (1, AUX_MOVE, gamma_coef)):
        rows[out, 0:OWN, :] = rows_base[out, 0:OWN, :] - moved0 * direction0
        rows[out, OWN:2 * OWN, :] = rows_base[out, OWN:2 * OWN, :] - moved0 * shared - moved1 * direction1
    for step in range(STEPS):
        copies = []
        for out, target in enumerate((pri_out, aux_out)):
            for i in range(OWN):
                at = step * OWN + i
                copies.append(
                    pltpu.make_async_copy(
                        rows.at[out, pl.ds(at, 1), :],
                        target.at[pl.ds(own_row(idx, step, i), 1), :],
                        sems.at[out, i],
                    )
                )
                copies[-1].start()
        for copy in copies:
            copy.wait()


def finish(indices, grads, own_grad, factors, spectrum, cross_values, rows_base, pri_base, aux_base):
    vmem = pl.BlockSpec(memory_space=pltpu.VMEM)
    anywhere = pl.BlockSpec(memory_space=pl.ANY)
    return pl.pallas_call(
        finish_kernel,
        out_shape=(jax.ShapeDtypeStruct((ROWS, OUT), jnp.float32),) * 2,
        in_specs=[pl.BlockSpec(memory_space=pltpu.SMEM)] + [vmem] * 7 + [anywhere] * 2,
        out_specs=(anywhere, anywhere),
        input_output_aliases={8: 0, 9: 1},
        scratch_shapes=[
            pltpu.VMEM((2, STEPS * OWN, OUT), jnp.float32),
            pltpu.SemaphoreType.DMA((2, OWN)),
        ],
        compiler_params=pltpu.CompilerParams(vmem_limit_bytes=16 * MIB),
        name="finish",
    )(indices, *grads, own_grad, factors, spectrum, cross_values, rows_base, pri_base, aux_base)


def on_device(features, targets, primary, auxiliary, factors, spectrum, indices):
    core = lax.axis_index("core")
    swap = lambda x: lax.ppermute(x, "core", [(0, 1), (1, 0)])
    exchange = lambda x: lax.all_to_all(x, SAME_CORE, 0, 0, tiled=True)

    send = pick(indices, features)
    other_features = swap(features)
    blend_bf, extra, pri_base, aux_base, rows_base = prepare(indices, targets, primary, auxiliary)
    other_blend = swap(blend_bf)
    by_core = indices.reshape(STEPS, CHIPS, 2, OWN).astype(jnp.float32)
    tiles = CHIPS // TILE_CHIPS
    halves = [lax.dynamic_index_in_dim(by_core, at, 2, False) for at in (core, 1 - core)]
    idx_halves = jnp.stack(halves).reshape(2, STEPS, tiles, TILE_CHIPS * OWN)

    block = exchange(send).reshape(CHIPS, STEPS, OWN, D)
    other_block = swap(block)
    partial = products(block, (features, other_features), (blend_bf, other_blend))
    received = exchange(partial.reshape(CHIPS, STEPS * OWN, OUT))
    cross_values, token = cross(block, other_block, idx_halves)
    own_grad, tosend = collect(received, extra, token)
    grads = exchange(tosend)
    return finish(
        indices,
        (grads, swap(grads)),
        own_grad,
        factors.reshape(STEPS, CHIPS, 2, OWN, D),
        spectrum,
        cross_values,
        rows_base,
        pri_base,
        aux_base,
    )


def solution(mesh):
    inner = Mesh(mesh.devices.reshape(mesh.shape["row"], mesh.shape["col"] // 2, 2), ALL)
    rows = P(ALL, None)
    return jax.shard_map(
        on_device,
        mesh=inner,
        in_specs=(rows, rows, rows, rows, P(), P(), P()),
        out_specs=(rows, rows),
        check_vma=False,
    )
```

time: 1760 us -> 136 us (0.08)
  waiting for transfers between devices: 1660 us -> 24.6 us
  Pallas kernels: 0 us -> 53.5 us
  matrix products: 35.9 us -> 0 us
  starting transfers between devices: 0.25 us -> 24.3 us
  other arithmetic: 24 us -> 0.02 us
  blocking collectives: 0 us -> 21.6 us
    reduce_scatter x2 -> x0, waiting for transfers between devices: 1250 us -> none  [on_device(): lax.psum_scatter(kernel_term(block, features, row_norms, blend_bf), ('row...]
    psum x2 -> x0, waiting for transfers between devices: 288 us -> none  [reduce_factor(): return lax.psum(partial_value, ('row', 'col'))]
    all_gather x2 -> x0, waiting for transfers between devices: 125 us -> none  [on_device(): block = lax.all_gather(own_feat, ('row', 'col'), axis=0, tiled=True)]
    pallas_call x0 -> x6, Pallas kernels: none -> 53.5 us  [the longest x1 24.8 us: products(): pl.pallas_call(product_kernel, grid=(STEPS, tiles), out_shape=jax.ShapeDt...]
    dot_general x12 -> x0, matrix products: 35.9 us -> none  [the longest x8 30 us: kernel_rows(): return jnp.dot(kernel, blend_bf, preferred_element_type=jnp.float32)]
    all_to_all x0 -> x2, waiting for transfers between devices: none -> 23.1 us  [on_device(): exchange = lambda x: lax.all_to_all(x, SAME_CORE, 0, 0, tiled=True)]
    all_to_all x0 -> x1, blocking collectives: none -> 21.6 us  [on_device(): exchange = lambda x: lax.all_to_all(x, SAME_CORE, 0, 0, tiled=True)]
    all_to_all x0 -> x2, starting transfers between devices: none -> 18.3 us  [on_device(): exchange = lambda x: lax.all_to_all(x, SAME_CORE, 0, 0, tiled=True)]
  transfers between devices with their start and end apart: 6 -> 6, of which waited for: 6 -> 2; matrix products, arithmetic and copies ran while one was open for 1% -> 1% of each run, Pallas kernels for 0% -> 31%
where the time goes in v1:
time: 136 us
  Pallas kernels  53.5 us (39%)
  waiting for transfers between devices  24.6 us (18%)
  starting transfers between devices  24.3 us (18%)
  blocking collectives  21.6 us (16%)
  local copies, waits for them, and re-layouts  10.6 us (8%)
    pallas_call x1, Pallas kernels, products(): pl.pallas_call(product_kernel, grid=(STEPS, tiles), out_shape=jax.ShapeDt...  24.8 us
    all_to_all x2, waiting for transfers between devices, on_device(): exchange = lambda x: lax.all_to_all(x, SAME_CORE, 0, 0, tiled=True)  23.1 us
    all_to_all x1, blocking collectives, on_device(): exchange = lambda x: lax.all_to_all(x, SAME_CORE, 0, 0, tiled=True)  21.6 us
    all_to_all x2, starting transfers between devices, on_device(): exchange = lambda x: lax.all_to_all(x, SAME_CORE, 0, 0, tiled=True)  18.3 us
    pallas_call x1, Pallas kernels, cross(): pl.pallas_call(cross_kernel, grid=(2, tiles), out_shape=(jax.ShapeDtypeSt...  13.9 us
    unnamed x18, local copies, waits for them, and re-layouts  9.82 us
    pallas_call x1, Pallas kernels, finish(): pl.pallas_call(finish_kernel, out_shape=(jax.ShapeDtypeStruct((ROWS, OUT)...  6.86 us
    ppermute x4, starting transfers between devices, on_device(): swap = lambda x: lax.ppermute(x, 'core', [(0, 1), (1, 0)])  6.02 us
  transfers between devices with their start and end apart: 6, of which 2 were waited for; matrix products, arithmetic and copies ran while one was open for 1% of the time, Pallas kernels for 31%

profile of v1, /device:TPU:1, one launch (start us, length us, event | category | flops | bytes accessed | tf_op | source)
XLA Modules:
  0.0 135.6 jit_solution(6170865758707240849)
XLA Ops:
  0.6 4.3 %pick.1 = bf16[64,32,512]{2,1,0:T(8,128)(2,1)} custom-call(s32[2,2048]{1,0:T(2,128)} %idx.5, bf16[2048,512]{1,0:T(8,128)(2,1)} %feat0.1), custom_call_target="tpu_custom_call" | custom-call | tf_op jit(solution)/shard_map/pick/pallas_call | solution.py:86
  5.0 0.0 copy-start.3
  5.0 0.0 copy-start.4
  5.0 0.0 copy-start.5
  5.0 0.0 copy-start.6
  5.0 12.4 %all-to-all-start = ((bf16[64,32,512]{2,1,0:T(8,128)(2,1)}), bf16[64,32,512]{2,1,0:T(8,128)(2,1)}, u32[]{:S(2)}, u32[]{:S(2)}) async-start(bf16[64,32,512]{2,1,0:T(8,128)(2,1)} %pick.1), calls=%async_computation | async-start | bytes 4194304 | tf_op jit(solution)/shard_map/all_to_all | solution.py:404
  17.4 1.0 collective-permute-start
  18.4 0.0 copy-done.3
  18.4 0.0 copy-done.4
  18.4 0.0 copy-done.5
  18.4 0.0 copy-done.6
  18.4 3.5 %prepare.1 = (bf16[2,2048,128]{2,1,0:T(8,128)(2,1)}, f32[32,128]{1,0:T(8,128)S(1)}, f32[2048,128]{1,0:T(8,128)}, f32[2048,128]{1,0:T(8,128)}, f32[2,32,128]{2,1,0:T(8,128)S(1)}) custom-call(s32[2,2048]{1,0:T(2,128)S(1)} %copy-done.6, bf16[2048,128]{1,0:T(8,128)(2,1)S(1)} %copy-done.5, f32[2048,128]{1,0:T(8,128)S(1)} %copy-done.3, f32[2048,128]{1,0:T(8,128)S(1)} %copy-done.4), custom_call_target="tpu_custom_call" | custom-call | tf_op jit(solution)/shard_map/prepare/pallas_call | solution.py:124
  21.9 0.0 collective-permute-start.1
  22.0 23.1 %all-to-all-done = bf16[64,32,512]{2,1,0:T(8,128)(2,1)} async-done(((bf16[64,32,512]{2,1,0:T(8,128)(2,1)}), bf16[64,32,512]{2,1,0:T(8,128)(2,1)}, u32[]{:S(2)}, u32[]{:S(2)}) %all-to-all-start) | async-done | bytes 2097184 | tf_op jit(solution)/shard_map/all_to_all | solution.py:404
  45.1 2.7 %collective-permute-start.2 = (bf16[64,2,16,512]{3,2,1,0:T(8,128)(2,1)}, bf16[64,2,16,512]{3,2,1,0:T(8,128)(2,1)}, u32[]{:S(2)}, u32[]{:S(2)}) collective-permute-start(bf16[64,2,16,512]{3,2,1,0:T(8,128)(2,1)} %bitcast.block_ref.own1.own0), channel_id=1, source_target_pairs={{0,1},{1,0},{2,3},{3,2},{4,5},{5,4},{6,7},{7,6},{8,9},{9,8},{10,11... | collective-permute-start | bytes 6291464 | tf_op jit(solution)/shard_map/ppermute | solution.py:403
  47.8 0.0 collective-permute-done.1.blend1
  47.8 0.0 copy-start.8
  47.8 0.0 collective-permute-done.feat1
  47.8 1.0 copy-done.8
  48.8 24.8 %products.1 = f32[64,2,16,128]{3,2,1,0:T(8,128)} custom-call(bf16[64,2,16,512]{3,2,1,0:T(8,128)(2,1)} %bitcast.block_ref.own1.own0, bf16[2048,512]{1,0:T(8,128)(2,1)} %feat0.1, bf16[2048,512]{1,0:T(8,128)(2,1)} %collective-permute-done.feat1, bf16[2,2048,128]{2,1,0:T(8,128)(2,1)} %get-tuple-element.11.blend0, bf16[2,2048,128]{2,1,0:T(8,128)(2,1)} %copy-done.8), custom_call_target="tpu_custom_call" | custom-call | flops 10737418240 | bytes 9437184 | tf_op jit(solution)/shard_map/products/pallas_call | solution.py:197
  73.7 5.9 %all-to-all-start.1 = ((f32[64,32,128]{2,1,0:T(8,128)}), f32[64,32,128]{2,1,0:T(8,128)S(1)}, u32[]{:S(2)}, u32[]{:S(2)}) async-start(f32[64,32,128]{2,1,0:T(8,128)} %bitcast.4), calls=%async_computation.1 | async-start | bytes 2097152 | tf_op jit(solution)/shard_map/all_to_all | solution.py:404
  79.6 0.2 convert_element_type.7
  79.8 0.4 dynamic-slice_reduce_fusion.1
  80.2 0.1 stack.9
  80.3 0.1 stack.10
  80.4 0.0 collective-permute-done.2.other1.other0
  80.5 13.9 %cross.1 = (bf16[2,64,16,2048]{3,2,1,0:T(8,128)(2,1)S(1)}, f32[8,128]{1,0:T(8,128)S(1)}) custom-call(f32[2,2,4,256]{3,2,1,0:T(4,128)S(1)} %pad_maximum_fusion.idx_ref, bf16[64,2,16,512]{3,2,1,0:T(8,128)(2,1)} %bitcast.block_ref.own1.own0, bf16[64,2,16,512]{3,2,1,0:T(8,128)(2,1)} %collective-permute-done.2.other1.other0, ...), custom_call_target="tpu_custom_call" | custom-call | flops 4294967296 | bytes 12582912 | tf_op jit(solution)/shard_map/cross/pallas_call | solution.py:242
  94.3 0.0 copy-start
  94.3 3.2 %copy-done = bf16[2,64,16,2048]{3,2,1,0:T(8,128)(2,1)} copy-done((bf16[2,64,16,2048]{3,2,1,0:T(8,128)(2,1)}, bf16[2,64,16,2048]{3,2,1,0:T(8,128)(2,1)S(1)}, u32[]{:S(2)}) %copy-start) | copy-done | bytes 8388632
  97.6 0.0 copy-start.7
  97.6 0.0 all-to-all-done.1.received
  97.6 0.1 collect.1
  97.7 21.6 %all_to_all.15.grads_own = bf16[64,32,128]{2,1,0:T(8,128)(2,1)S(1)} all-to-all(bf16[64,32,128]{2,1,0:T(8,128)(2,1)S(1)} %get-tuple-element.14), channel_id=1, replica_groups=mesh['row'=16,'y'=4,'core'=2] {'row','y'}, dimensions={0} | all-to-all | bytes 1048576 | tf_op jit(solution)/shard_map/all_to_all | solution.py:404
  119.3 2.2 %collective-permute-start.3 = (bf16[64,32,128]{2,1,0:T(8,128)(2,1)S(1)}, bf16[64,32,128]{2,1,0:T(8,128)(2,1)S(1)}, u32[]{:S(2)}, u32[]{:S(2)}) collective-permute-start(bf16[64,32,128]{2,1,0:T(8,128)(2,1)S(1)} %all_to_all.15.grads_own), channel_id=1, source_target_pairs={{0,1},{1,0},{2,3},{3,2},{4,5},{5,4},{6,7},{7,6},{8,9},{9,8},{10,11... | collective-permute-start | bytes 1572872 | tf_op jit(solution)/shard_map/ppermute | solution.py:403
  121.5 1.5 %collective-permute-done.3.grads_other = bf16[64,32,128]{2,1,0:T(8,128)(2,1)S(1)} collective-permute-done((bf16[64,32,128]{2,1,0:T(8,128)(2,1)S(1)}, bf16[64,32,128]{2,1,0:T(8,128)(2,1)S(1)}, u32[]{:S(2)}, u32[]{:S(2)}) %collective-permute-start.3) | collective-permute-done | bytes 524320 | tf_op jit(solution)/shard_map/ppermute | solution.py:403
  123.0 0.0 copy-done.7
  123.0 0.0 copy-start.1
  123.0 3.4 %copy-done.1 = bf16[2,64,16,2048]{3,2,1,0:T(8,128)(2,1)S(1)} copy-done((bf16[2,64,16,2048]{3,2,1,0:T(8,128)(2,1)S(1)}, bf16[2,64,16,2048]{3,2,1,0:T(8,128)(2,1)}, u32[]{:S(2)}) %copy-start.1) | copy-done | bytes 8388632
  126.4 0.0 copy-start.2
  126.4 2.2 %copy-done.2 = bf16[2,2048,512]{2,1,0:T(8,128)(2,1)S(1)} copy-done((bf16[2,2048,512]{2,1,0:T(8,128)(2,1)S(1)}, bf16[2,2048,512]{2,1,0:T(8,128)(2,1)}, u32[]{:S(2)}) %copy-start.2) | copy-done | bytes 4194328
  128.6 6.9 %finish.1 = (f32[2048,128]{1,0:T(8,128)}, f32[2048,128]{1,0:T(8,128)}) custom-call(s32[2,2048]{1,0:T(2,128)S(1)} %copy-done.6, bf16[64,32,128]{2,1,0:T(8,128)(2,1)S(1)} %all_to_all.15.grads_own, bf16[64,32,128]{2,1,0:T(8,128)(2,1)S(1)} %collective-permute-done.3.grads_other, ...), custom_call_target="tpu_custom_call", output_to_operand_aliasing={{0}: (8, {}), {1}: (9, {})} | custom-call | tf_op jit(solution)/shard_map/finish/pallas_call | solution.py:386
  (2 shorter events, 0.0 us)
Async XLA Ops:
  5.0 13.5 %copy-start.3 = (f32[2048,128]{1,0:T(8,128)S(1)}, f32[2048,128]{1,0:T(8,128)}, u32[]{:S(2)}) copy-start(f32[2048,128]{1,0:T(8,128)} %pri.1) | copy-start | bytes 3145732
  5.0 13.5 %copy-start.4 = (f32[2048,128]{1,0:T(8,128)S(1)}, f32[2048,128]{1,0:T(8,128)}, u32[]{:S(2)}) copy-start(f32[2048,128]{1,0:T(8,128)} %aux.1) | copy-start | bytes 3145732
  5.0 13.4 %copy-start.5 = (bf16[2048,128]{1,0:T(8,128)(2,1)S(1)}, bf16[2048,128]{1,0:T(8,128)(2,1)}, u32[]{:S(2)}) copy-start(bf16[2048,128]{1,0:T(8,128)(2,1)} %tgt.1) | copy-start | bytes 1572868
  5.0 13.4 %copy-start.6 = (s32[2,2048]{1,0:T(2,128)S(1)}, s32[2,2048]{1,0:T(2,128)}, u32[]{:S(2)}) copy-start(s32[2,2048]{1,0:T(2,128)} %idx.5) | copy-start | bytes 49156
  5.0 40.1 %all-to-all-start = ((bf16[64,32,512]{2,1,0:T(8,128)(2,1)}), bf16[64,32,512]{2,1,0:T(8,128)(2,1)}, u32[]{:S(2)}, u32[]{:S(2)}) async-start(bf16[64,32,512]{2,1,0:T(8,128)(2,1)} %pick.1), calls=%async_computation | async-start | bytes 4194304 | tf_op jit(solution)/shard_map/all_to_all | solution.py:404
  17.4 30.4 %collective-permute-start = (bf16[2048,512]{1,0:T(8,128)(2,1)}, bf16[2048,512]{1,0:T(8,128)(2,1)}, u32[]{:S(2)}, u32[]{:S(2)}) collective-permute-start(bf16[2048,512]{1,0:T(8,128)(2,1)} %feat0.1), channel_id=1, source_target_pairs={{0,1},{1,0},{2,3},{3,2},{4,5},{5,4},{6,7},{7,6},{8,9},{9,8},{10,11... | collective-permute-start | bytes 6291464 | tf_op jit(solution)/shard_map/ppermute | solution.py:403
  21.9 25.9 %collective-permute-start.1 = (bf16[2,2048,128]{2,1,0:T(8,128)(2,1)}, bf16[2,2048,128]{2,1,0:T(8,128)(2,1)S(1)}, u32[]{:S(2)}, u32[]{:S(2)}) collective-permute-start(bf16[2,2048,128]{2,1,0:T(8,128)(2,1)} %get-tuple-element.11.blend0), channel_id=1, source_target_pairs={{0,1},{1,0},{2,3},{3,2},{4,5},{5,4},{6,7},{7,6},{8,9},{9,8},{10,11... | collective-permute-start | bytes 3145736 | tf_op jit(solution)/shard_map/ppermute | solution.py:403
  45.1 35.4 %collective-permute-start.2 = (bf16[64,2,16,512]{3,2,1,0:T(8,128)(2,1)}, bf16[64,2,16,512]{3,2,1,0:T(8,128)(2,1)}, u32[]{:S(2)}, u32[]{:S(2)}) collective-permute-start(bf16[64,2,16,512]{3,2,1,0:T(8,128)(2,1)} %bitcast.block_ref.own1.own0), channel_id=1, source_target_pairs={{0,1},{1,0},{2,3},{3,2},{4,5},{5,4},{6,7},{7,6},{8,9},{9,8},{10,11... | collective-permute-start | bytes 6291464 | tf_op jit(solution)/shard_map/ppermute | solution.py:403
  47.8 1.0 copy-start.8
  73.7 23.9 %all-to-all-start.1 = ((f32[64,32,128]{2,1,0:T(8,128)}), f32[64,32,128]{2,1,0:T(8,128)S(1)}, u32[]{:S(2)}, u32[]{:S(2)}) async-start(f32[64,32,128]{2,1,0:T(8,128)} %bitcast.4), calls=%async_computation.1 | async-start | bytes 2097152 | tf_op jit(solution)/shard_map/all_to_all | solution.py:404
  94.3 3.2 %copy-start = (bf16[2,64,16,2048]{3,2,1,0:T(8,128)(2,1)}, bf16[2,64,16,2048]{3,2,1,0:T(8,128)(2,1)S(1)}, u32[]{:S(2)}) copy-start(bf16[2,64,16,2048]{3,2,1,0:T(8,128)(2,1)S(1)} %get-tuple-element.16.cross_ref) | copy-start | bytes 25165828
  97.6 25.5 %copy-start.7 = (f32[2,512]{1,0:T(2,128)S(1)}, f32[2,512]{1,0:T(2,128)}, u32[]{:S(2)}) copy-start(f32[2,512]{1,0:T(2,128)} %spectrum.1) | copy-start | bytes 12292
  119.3 3.8 %collective-permute-start.3 = (bf16[64,32,128]{2,1,0:T(8,128)(2,1)S(1)}, bf16[64,32,128]{2,1,0:T(8,128)(2,1)S(1)}, u32[]{:S(2)}, u32[]{:S(2)}) collective-permute-start(bf16[64,32,128]{2,1,0:T(8,128)(2,1)S(1)} %all_to_all.15.grads_own), channel_id=1, source_target_pairs={{0,1},{1,0},{2,3},{3,2},{4,5},{5,4},{6,7},{7,6},{8,9},{9,8},{10,11... | collective-permute-start | bytes 1572872 | tf_op jit(solution)/shard_map/ppermute | solution.py:403
  123.0 3.4 %copy-start.1 = (bf16[2,64,16,2048]{3,2,1,0:T(8,128)(2,1)S(1)}, bf16[2,64,16,2048]{3,2,1,0:T(8,128)(2,1)}, u32[]{:S(2)}) copy-start(bf16[2,64,16,2048]{3,2,1,0:T(8,128)(2,1)} %copy-done) | copy-start | bytes 25165828
  126.4 2.2 %copy-start.2 = (bf16[2,2048,512]{2,1,0:T(8,128)(2,1)S(1)}, bf16[2,2048,512]{2,1,0:T(8,128)(2,1)}, u32[]{:S(2)}) copy-start(bf16[2,2048,512]{2,1,0:T(8,128)(2,1)} %param.11) | copy-start | bytes 12582916

commit v2 on v1

v2 whole, which is shorter than its diff:
```python
import functools

import jax
import jax.numpy as jnp
from jax import lax
from jax.experimental import pallas as pl
from jax.experimental.pallas import tpu as pltpu
from jax.sharding import Mesh, PartitionSpec as P

STEPS = 2
CHIPS = 64
OWN = 16
ROWS = 2048
D = 512
OUT = 128
LOG2E = 1.4426950408889634
MIB = 1024 * 1024
ALL = ("row", "y", "core")
LINE = 16
Y = 4
CHUNK = 512
GROUP = 16
REPEAT = 8
WIDE = 32

ridge_coef = 0.5
shift_rho = 1.0
step_eta = 0.5
beta_coef = 0.8
gamma_coef = 0.3
alpha_coef = 0.6

MOVE = alpha_coef * gamma_coef + (1.0 - alpha_coef) * step_eta
AUX_MOVE = beta_coef * gamma_coef + (1.0 - beta_coef) * MOVE


def chip_index():
    return lax.axis_index("row") * lax.axis_size("y") + lax.axis_index("y")


def nt(a, b):
    return lax.dot_general(a, b, (((1,), (1,)), ((), ())), preferred_element_type=jnp.float32)


def blends(aux, pri):
    blend0 = alpha_coef * aux + (1.0 - alpha_coef) * pri
    aux1 = beta_coef * aux + (1.0 - beta_coef) * blend0
    blend1 = alpha_coef * aux1 + (1.0 - alpha_coef) * blend0
    return blend0, aux1, blend1


def place():
    return lax.axis_index("y") * LINE + lax.axis_index("row")


def own_row(idx, step, i):
    position = chip_index() * 2 + lax.axis_index("core")
    return idx[step, position * OWN + i] - position * ROWS


def pick_kernel(idx, feat, send, near, rows_ref, sem, send_sem):
    copies = []
    which = lax.broadcasted_iota(jnp.int32, (STEPS * OWN, 1), 0)
    column = jnp.zeros((STEPS * OWN, 1), jnp.int32)
    for at in range(STEPS * OWN):
        row = own_row(idx, at // OWN, at % OWN)
        inside = lax.bitwise_and(row, GROUP - 1)
        first = pl.multiple_of(row - inside, GROUP)
        copies.append(
            pltpu.make_async_copy(
                feat.at[pl.ds(first, GROUP), :], near.at[pl.ds(at * GROUP, GROUP), :], sem.at[at]
            )
        )
        copies[-1].start()
        column = jnp.where(which == at, at * GROUP + inside, column)
    chosen = lax.broadcasted_iota(jnp.int32, (STEPS * OWN, STEPS * OWN * GROUP), 1) == column
    chosen = chosen.astype(jnp.float32).astype(jnp.bfloat16)
    for copy in copies:
        copy.wait()
    rows = jnp.dot(chosen, near[...], preferred_element_type=jnp.float32)
    rows_ref[...] = jnp.broadcast_to(rows.astype(jnp.bfloat16)[None], rows_ref.shape)
    copies = [
        pltpu.make_async_copy(rows_ref, send.at[pl.ds(at * REPEAT, REPEAT)], send_sem.at[at])
        for at in range(LINE // REPEAT)
    ]
    for copy in copies:
        copy.start()
    for copy in copies:
        copy.wait()


def pick(indices, features):
    return pl.pallas_call(
        pick_kernel,
        out_shape=jax.ShapeDtypeStruct((LINE, STEPS * OWN, D), jnp.bfloat16),
        in_specs=[pl.BlockSpec(memory_space=pltpu.SMEM), pl.BlockSpec(memory_space=pltpu.HBM)],
        out_specs=pl.BlockSpec(memory_space=pltpu.HBM),
        scratch_shapes=[
            pltpu.VMEM((STEPS * OWN * GROUP, D), jnp.bfloat16),
            pltpu.VMEM((REPEAT, STEPS * OWN, D), jnp.bfloat16),
            pltpu.SemaphoreType.DMA((STEPS * OWN,)),
            pltpu.SemaphoreType.DMA((LINE // REPEAT,)),
        ],
        compiler_params=pltpu.CompilerParams(vmem_limit_bytes=58 * MIB),
        name="pick",
    )(indices, features)


def prepare_kernel(idx, tgt, pri, aux, blend_bf, extra):
    blend0, _, blend1 = blends(aux[...], pri[...])
    blend_bf[:, :OUT] = blend0.astype(jnp.bfloat16)
    blend_bf[:, OUT:] = blend1.astype(jnp.bfloat16)
    which = lax.broadcasted_iota(jnp.int32, (STEPS * OWN, 1), 0)
    column = jnp.zeros((STEPS * OWN, 1), jnp.int32)
    for at in range(STEPS * OWN):
        row = own_row(idx, at // OWN, at % OWN)
        column = jnp.where(which == at, row, column)
        here, _, here1 = blends(aux[pl.ds(row, 1), :], pri[pl.ds(row, 1), :])
        extra[pl.ds(at, 1), :] = ridge_coef * (here1 if at >= OWN else here)
    chosen = lax.broadcasted_iota(jnp.int32, (STEPS * OWN, ROWS), 1) == column
    chosen = chosen.astype(jnp.float32).astype(jnp.bfloat16)
    extra[...] -= jnp.dot(chosen, tgt[...], preferred_element_type=jnp.float32)


def prepare(indices, targets, primary, auxiliary):
    vmem = pl.BlockSpec(memory_space=pltpu.VMEM)
    return pl.pallas_call(
        prepare_kernel,
        out_shape=(
            pltpu.HBM((ROWS, STEPS * OUT), jnp.bfloat16),
            jax.ShapeDtypeStruct((STEPS * OWN, OUT), jnp.float32),
        ),
        in_specs=[pl.BlockSpec(memory_space=pltpu.SMEM)] + [vmem] * 3,
        out_specs=(vmem,) * 2,
        compiler_params=pltpu.CompilerParams(vmem_limit_bytes=16 * MIB),
        name="prepare",
    )(indices, targets, primary, auxiliary)


SCALE = LOG2E / (2.0 * D)


def row_norms(block):
    wide = block.astype(jnp.float32)
    return jnp.sum(wide * wide, axis=1, keepdims=True) * SCALE


def kernel_values(block, block_norms, feat, feat_norms):
    return jnp.exp2(nt(block, feat) * (2.0 * SCALE) - (block_norms + feat_norms))


def norm_row(feat, scale=SCALE):
    wide = feat.astype(jnp.float32)
    wide = wide * wide
    lanes = wide[:, :128]
    for at in range(128, D, 128):
        lanes += wide[:, at:at + 128]
    return jnp.sum(jnp.transpose(lanes), axis=0, keepdims=True) * scale


def product_kernel(*refs, pieces, sums, others, first):
    blocks, (feat0, feat1, blend0, blend1), rest = refs[:pieces], refs[pieces:pieces + 4], refs[pieces + 4:]
    if not first:
        norms_ref, *rest = rest
    back, rest = rest[:sums], rest[sums:]
    copies = []
    if others:
        sources, (out, whole, sems) = rest[:others], rest[others:]
        y = lax.axis_index("y")
        at = 0
        for source, (delta, first) in zip(sources, ((0, 0), (-1, 0), (1, 0), (2, 0), (2, LINE // 2))):
            target = whole.at[lax.bitwise_and(y + delta, Y - 1), pl.ds(first, source.shape[0])]
            copies.append(pltpu.make_async_copy(source, target, sems.at[at]))
            copies[-1].start()
            at += 1
    elif first:
        out, norms_ref = rest
    else:
        out, = rest
    count = LINE * STEPS * OWN
    block = jnp.concatenate([piece[...].reshape(-1, D) for piece in blocks], axis=0)
    norms = row_norms(block)
    total = jnp.zeros((count, STEPS * OUT), jnp.float32)
    behind = None
    for part in [(which, at) for which in range(2) for at in range(0, ROWS, CHUNK)] + [None]:
        ahead = None
        if part is not None:
            which, at = part
            span = pl.ds(at, CHUNK)
            feat = (feat0, feat1)[which][span, :]
            if first:
                norms_ref[which:which + 1, span] = norm_row(feat)
            kernel = kernel_values(block, norms, feat, norms_ref[which:which + 1, span])
            ahead = (kernel.astype(jnp.bfloat16), (blend0, blend1)[which][span, :])
        if behind is not None:
            total += jnp.dot(*behind, preferred_element_type=jnp.float32)
        behind = ahead
    row = lax.broadcasted_iota(jnp.int32, (count, 1), 0)
    first_step = lax.bitwise_and(row, OWN) == 0
    result = jnp.where(first_step, total[:, :OUT], total[:, OUT:]).reshape(out.shape)
    for part in back:
        result += part[...].astype(jnp.float32)
    out[...] = result.astype(out.dtype)
    for copy in copies:
        copy.wait()


def products(pieces, features, blend_bf, norms=(), sums=(), others=()):
    vmem = pl.BlockSpec(memory_space=pltpu.VMEM)
    far = pl.BlockSpec(memory_space=pltpu.HBM)
    shape = (LINE, STEPS * OWN, OUT)
    out_shape = [jax.ShapeDtypeStruct(shape, jnp.float32) if others else pltpu.HBM(shape, jnp.bfloat16)]
    if not norms:
        out_shape.append(jax.ShapeDtypeStruct((2, ROWS), jnp.float32))
    if others:
        out_shape.append(pltpu.HBM((Y, LINE, STEPS * OWN, D), jnp.bfloat16))
    return pl.pallas_call(
        functools.partial(product_kernel, pieces=len(pieces), sums=len(sums), others=len(others), first=not norms),
        out_shape=tuple(out_shape),
        in_specs=[vmem] * (len(pieces) + 4 + len(norms) + len(sums) + len(others)),
        out_specs=(vmem, far if others else vmem)[: len(out_shape)],
        scratch_shapes=[pltpu.SemaphoreType.DMA((len(others),))] if others else [],
        compiler_params=pltpu.CompilerParams(vmem_limit_bytes=16 * MIB),
        cost_estimate=pl.CostEstimate(
            flops=2 * 512 * 4096 * 768, bytes_accessed=MIB, transcendentals=512 * 4096
        ),
        name="products",
    )(*pieces, *features, *blend_bf, *norms, *sums, *others)


def cross_kernel(
    idx, idx_ref, own0, other0, own1, other1, factors, after, weights, own_rows, factor_ref, norms_ref, sems
):
    half = pl.program_id(0)
    tile = pl.program_id(1)
    opening = jnp.logical_and(half == 0, tile == 0)
    core = lax.axis_index("core")
    size = WIDE * OWN
    ones = (own1, other1)
    parts = [(which, at) for which in range(2) for at in range(0, CHIPS, WIDE)]

    def loads(which):
        return [
            pltpu.make_async_copy(
                factors.at[1, :, y, lax.bitwise_xor(core, which)],
                factor_ref.at[which, pl.ds(y * LINE, LINE)],
                sems.at[which, y],
            )
            for y in range(Y)
        ]

    def tile_of(first_tile):
        if first_tile:
            for load in loads(0) + loads(1):
                load.start()
        block = jnp.where(half == 0, own0[...], other0[...]).reshape(size, D)
        norms = row_norms(block)
        here = idx_ref[pl.ds(half, 1), 0, pl.ds(tile, 1), :].reshape(1, size)
        left = jnp.transpose(jnp.broadcast_to(here, (size, size)))
        total = jnp.zeros((size, D), jnp.float32)
        behind = None
        for at, part in enumerate(parts + [None]):
            ahead = None
            if part is not None:
                which, first = part
                feat = ones[which][first:first + WIDE, 0].reshape(size, D)
                if first_tile:
                    norms_ref[at:at + 1, :] = norm_row(feat)
                kernel = kernel_values(block, norms, feat, norms_ref[at:at + 1, :])
                right = idx_ref[which, 1, first // WIDE].reshape(1, size)
                kernel += jnp.where(left == right, ridge_coef, 0.0)
                ahead = (kernel.astype(jnp.bfloat16), which, first)
            if behind is not None:
                values, which, first = behind
                if first_tile and first == 0:
                    for load in loads(which):
                        load.wait()
                factor = factor_ref[which, first:first + WIDE].reshape(size, D)
                total += jnp.dot(values, factor, preferred_element_type=jnp.float32)
            behind = ahead
        weights[...] = total.astype(jnp.bfloat16)

    pl.when(opening)(lambda: tile_of(True))
    pl.when(jnp.logical_not(opening))(lambda: tile_of(False))

    block = jnp.where(half == 0, own0[...], other0[...]).reshape(size, D)
    here = idx_ref[pl.ds(half, 1), 0, pl.ds(tile, 1), :].reshape(1, size)
    mine = own1[place(), 0]
    which_row = lax.broadcasted_iota(jnp.int32, (OWN, 1), 0)
    column = jnp.zeros((OWN, 1), jnp.int32)
    position = chip_index() * 2 + core
    for i in range(OWN):
        column = jnp.where(which_row == i, idx[1, position * OWN + i], column)
    kernel = kernel_values(mine, row_norms(mine), block, norm_row(block))
    kernel += jnp.where(column.astype(jnp.float32) == here, ridge_coef, 0.0)
    own_rows[...] = kernel.astype(jnp.bfloat16)


def cross(indices, own, other, idx, factors, after):
    tiles = CHIPS // WIDE
    tile_spec = pl.BlockSpec((WIDE, 1, OWN, D), lambda h, i: (i, 0, 0, 0))
    whole = pl.BlockSpec((CHIPS, 1, OWN, D), lambda h, i: (0, 1, 0, 0))
    anywhere = pl.BlockSpec(memory_space=pl.ANY)
    size = WIDE * OWN
    own, factors = [pltpu.with_memory_space_constraint(x, pltpu.HBM) for x in (own, factors)]
    return pl.pallas_call(
        cross_kernel,
        grid=(2, tiles),
        out_shape=(
            pltpu.HBM((ROWS, D), jnp.bfloat16),
            jax.ShapeDtypeStruct((OWN, ROWS), jnp.bfloat16),
        ),
        in_specs=[
            pl.BlockSpec(memory_space=pltpu.SMEM),
            pl.BlockSpec((2, STEPS, tiles, size), lambda h, i: (0, 0, 0, 0)),
            tile_spec, tile_spec, whole, whole, pl.BlockSpec(memory_space=pltpu.HBM), anywhere,
        ],
        out_specs=(
            pl.BlockSpec((size, D), lambda h, i: (h * tiles + i, 0)),
            pl.BlockSpec((OWN, size), lambda h, i: (0, h * tiles + i)),
        ),
        scratch_shapes=[
            pltpu.VMEM((2, CHIPS, OWN, D), jnp.bfloat16),
            pltpu.VMEM((2 * tiles, size), jnp.float32),
            pltpu.SemaphoreType.DMA((2, Y)),
        ],
        compiler_params=pltpu.CompilerParams(vmem_limit_bytes=48 * MIB),
        cost_estimate=pl.CostEstimate(
            flops=2 * 2048 * 2048 * 1024, bytes_accessed=8 * MIB, transcendentals=2048 * 2048
        ),
        name="cross",
    )(indices, idx, own, other, own, other, factors, after)


def collect_kernel(received, extra, own_grad, send):
    total = jnp.sum(received[...], axis=0) + extra[...]
    own_grad[...] = total
    send[...] = jnp.broadcast_to(total.astype(jnp.bfloat16)[None], send.shape)


def collect(received, extra):
    vmem = pl.BlockSpec(memory_space=pltpu.VMEM)
    return pl.pallas_call(
        collect_kernel,
        out_shape=(
            jax.ShapeDtypeStruct((STEPS * OWN, OUT), jnp.float32),
            jax.ShapeDtypeStruct((2 * CHIPS, STEPS * OWN, OUT), jnp.bfloat16),
        ),
        in_specs=[vmem, vmem],
        out_specs=(vmem, vmem),
        compiler_params=pltpu.CompilerParams(vmem_limit_bytes=8 * MIB),
        name="collect",
    )(received, extra)


def split(x):
    high = x.astype(jnp.bfloat16)
    return high, (x - high.astype(jnp.float32)).astype(jnp.bfloat16)


def split_nt(x, y):
    high, low = split(x)
    both = nt(jnp.concatenate([high, low], axis=0), y)
    return both[: x.shape[0]] + both[x.shape[0]:]


def finish_kernel(
    idx, grads, own_grad, own_cross, spectrum, factors, weights, pri, aux,
    pri_out, aux_out, result, factor_ref, weights_ref, sems, load_sems, factor_sems,
):
    chip = place()
    core = lax.axis_index("core")
    count = CHIPS * OWN
    loads = [
        pltpu.make_async_copy(
            factors.at[step, :, y, lax.bitwise_xor(core, half)],
            factor_ref.at[step, half, pl.ds(y * LINE, LINE)],
            factor_sems.at[step, half, y],
        )
        for step in range(STEPS) for half in range(2) for y in range(Y)
    ]
    loads.append(pltpu.make_async_copy(weights, weights_ref, load_sems.at[2]))
    for out, source in enumerate((pri, aux)):
        loads.append(pltpu.make_async_copy(source, result.at[out], load_sems.at[out]))
    for load in loads:
        load.start()
    coef = 1.0 / (spectrum[...] + shift_rho) - 1.0 / shift_rho

    def factor(step, half):
        return factor_ref[step, half].reshape(count, D)

    def gradient(step, half):
        other = lax.bitwise_xor(core, half)
        wide = [
            grads[:, y, other, step * OWN:(step + 1) * OWN, :].reshape(LINE * OWN, OUT) for y in range(Y)
        ]
        return jnp.transpose(jnp.concatenate(wide, axis=0).astype(jnp.float32))

    grad0 = [gradient(0, half) for half in range(2)]
    grad1 = [gradient(1, half) for half in range(2)]

    def project(grad, step):
        total = jnp.zeros((OUT, D), jnp.float32)
        for half in range(2):
            total += jnp.dot(
                grad[half].astype(jnp.bfloat16), factor(step, half), preferred_element_type=jnp.float32
            )
        return total

    for load in loads[:2 * Y]:
        load.wait()
    scaled0 = project(grad0, 0) * coef[0:1]
    moves = []
    for half in range(2):
        direction = grad0[half] / shift_rho + split_nt(scaled0, factor(0, half))
        moves.append((-MOVE * direction).astype(jnp.bfloat16))
    for load in loads[2 * Y:]:
        load.wait()
    projected = project(grad1, 1)
    _, aux1, blend1 = blends(result[1], result[0])
    result[0] = blend1
    result[1] = beta_coef * aux1 + (1.0 - beta_coef) * blend1
    for half in range(2):
        projected += jnp.dot(
            moves[half], weights_ref[half * count:(half + 1) * count, :], preferred_element_type=jnp.float32
        )
    scaled1 = projected * coef[1:2]

    own0 = own_grad[0:OWN, :]
    own1 = own_grad[OWN:2 * OWN, :]
    for half in range(2):
        own1 += nt(own_cross[:, half * count:(half + 1) * count], moves[half])

    def own_direction(step, grad, scaled):
        high, low = split(scaled)
        mine = factor_ref[step, 0, chip]
        return grad / shift_rho + nt(mine, high) + nt(mine, low)

    direction0 = own_direction(0, own0, scaled0)
    direction1 = own_direction(1, own1, scaled1)

    for step, direction, moved in (
        (0, direction0, (MOVE, AUX_MOVE)),
        (1, direction1, (step_eta, gamma_coef)),
    ):
        for i in range(OWN):
            row = pl.ds(own_row(idx, step, i), 1)
            for out in range(2):
                result[out, row, :] -= moved[out] * direction[i:i + 1, :]
    stores = []
    for out, target in enumerate((pri_out, aux_out)):
        for at in range(2):
            part = pl.ds(at * (ROWS // 2), ROWS // 2)
            stores.append(pltpu.make_async_copy(result.at[out, part, :], target.at[part, :], sems.at[out, at]))
            stores[-1].start()
    for store in stores:
        store.wait()


def finish(indices, grads, own_grad, own_cross, spectrum, factors, weights, primary, auxiliary):
    vmem = pl.BlockSpec(memory_space=pltpu.VMEM)
    factors, weights, primary, auxiliary = [
        pltpu.with_memory_space_constraint(x, pltpu.HBM) for x in (factors, weights, primary, auxiliary)
    ]
    far = pl.BlockSpec(memory_space=pltpu.HBM)
    return pl.pallas_call(
        finish_kernel,
        out_shape=(pltpu.HBM((ROWS, OUT), jnp.float32),) * 2,
        in_specs=[pl.BlockSpec(memory_space=pltpu.SMEM)] + [vmem] * 4 + [far] * 4,
        out_specs=(far, far),
        scratch_shapes=[
            pltpu.VMEM((2, ROWS, OUT), jnp.float32),
            pltpu.VMEM((STEPS, 2, CHIPS, OWN, D), jnp.bfloat16),
            pltpu.VMEM((ROWS, D), jnp.bfloat16),
            pltpu.SemaphoreType.DMA((2, 2)),
            pltpu.SemaphoreType.DMA((3,)),
            pltpu.SemaphoreType.DMA((STEPS, 2, Y)),
        ],
        compiler_params=pltpu.CompilerParams(vmem_limit_bytes=32 * MIB),
        name="finish",
    )(indices, grads, own_grad, own_cross, spectrum, factors, weights, primary, auxiliary)


def on_device(features, targets, primary, auxiliary, factors, spectrum, indices):
    core = lax.axis_index("core")
    swap = lambda x: lax.ppermute(x, "core", [(0, 1), (1, 0)])
    exchange = lambda x: lax.all_to_all(x, "row", 0, 0, tiled=True)

    def shift(x, by):
        return lax.ppermute(x, "y", [(y, (y + by) % Y) for y in range(Y)])

    send = pick(indices, features)
    other_features = swap(features)
    send, primary, auxiliary = lax.optimization_barrier((send, primary, auxiliary))
    here = exchange(send)
    blend_bf, extra = prepare(indices, targets, primary, auxiliary)
    blend_bf = (blend_bf, swap(blend_bf))
    features = (features, other_features)
    by_core = indices.reshape(STEPS, LINE, Y, 2, OWN).astype(jnp.float32)
    halves = [lax.dynamic_index_in_dim(by_core, at, 3, False) for at in (core, 1 - core)]
    idx_halves = jnp.stack(halves).transpose(0, 1, 3, 2, 4).reshape(2, STEPS, CHIPS // WIDE, WIDE * OWN)

    below = shift(here, 1)
    above = shift(here, -1)
    across = (shift(below[: LINE // 2], 1), shift(above[LINE // 2:], -1))
    to_below, norms = products((below,), features, blend_bf)
    norms = (norms,)
    for_below = shift(to_below, -1)
    above_late, _ = lax.optimization_barrier((above, to_below))
    to_above, = products((above_late,), features, blend_bf, norms)
    for_above = shift(to_above, 1)
    across_late, _ = lax.optimization_barrier((across, to_above))
    to_across, = products(across_late, features, blend_bf, norms)
    for_across = shift(to_across, 2)
    here_late, _ = lax.optimization_barrier((here, to_across))
    partial, block = products(
        (here_late,), features, blend_bf, norms, (for_below, for_above), (here, below, above) + across
    )
    partial = partial + for_across.astype(jnp.float32)
    block, partial = lax.optimization_barrier((block, partial))
    block = block.reshape(CHIPS, STEPS, OWN, D)
    other_block = swap(block)
    received = exchange(partial)
    own_grad, tosend = collect(received, extra)
    factors = factors.reshape(STEPS, LINE, Y, 2, OWN, D)
    weights, own_cross = cross(indices, block, other_block, idx_halves, factors, own_grad)
    grads = lax.all_to_all(tosend, ALL, 0, 0, tiled=True).reshape(LINE, Y, 2, STEPS * OWN, OUT)
    return finish(indices, grads, own_grad, own_cross, spectrum, factors, weights, primary, auxiliary)


def solution(mesh):
    inner = Mesh(mesh.devices.reshape(mesh.shape["row"], mesh.shape["col"] // 2, 2), ALL)
    rows = P(ALL, None)
    return jax.shard_map(
        on_device,
        mesh=inner,
        in_specs=(rows, rows, rows, rows, P(), P(), P()),
        out_specs=(rows, rows),
        check_vma=False,
    )
```

time: 136 us -> 115 us (0.85)
  local copies, waits for them, and re-layouts: 10.6 us -> 0.55 us
  Pallas kernels: 53.5 us -> 49.5 us
  blocking collectives: 21.6 us -> 18.4 us
  waiting for transfers between devices: 24.6 us -> 21.8 us
  starting transfers between devices: 24.3 us -> 22.6 us
    all_to_all x2, waiting for transfers between devices: 23.1 us -> 11.6 us  [the longest x1 8.1 us: on_device(): exchange = lambda x: lax.all_to_all(x, 'row', 0, 0, tiled=True)]
    ppermute x0 -> x7, waiting for transfers between devices: none -> 10.2 us  [shift(): return lax.ppermute(x, 'y', [(y, (y + by) % Y) for y in range(Y)])]
    unnamed x18 -> x16, local copies, waits for them, and re-layouts: 9.82 us -> 0.04 us
    all_to_all x2, starting transfers between devices: 18.3 us -> 9.11 us  [the longest x1 5.57 us: on_device(): lax.all_to_all(tosend, ALL, 0, 0, tiled=True)]
    ppermute x0 -> x7, starting transfers between devices: none -> 7.4 us  [shift(): return lax.ppermute(x, 'y', [(y, (y + by) % Y) for y in range(Y)])]
    pallas_call x5 -> x8, Pallas kernels: 53.4 us -> 48.5 us  [the longest x4 19.1 us: products(): pl.pallas_call(functools.partial(product_kernel, pieces=len(pieces), sums...]
    all_to_all x1, blocking collectives: 21.6 us -> 18.4 us  [on_device(): exchange = lambda x: lax.all_to_all(x, 'row', 0, 0, tiled=True)]
    ppermute x4 -> x3, waiting for transfers between devices: 1.54 us -> 0.01 us  [on_device(): swap = lambda x: lax.ppermute(x, 'core', [(0, 1), (1, 0)])]
  transfers between devices with their start and end apart: 6 -> 12, of which waited for: 2 -> 3; matrix products, arithmetic and copies ran while one was open for 1% -> 0% of each run, Pallas kernels for 31% -> 36%
where the time goes in v2:
time: 115 us
  Pallas kernels  49.5 us (43%)
  starting transfers between devices  22.6 us (20%)
  waiting for transfers between devices  21.8 us (19%)
  blocking collectives  18.4 us (16%)
    pallas_call x4, Pallas kernels, products(): pl.pallas_call(functools.partial(product_kernel, pieces=len(pieces), sums...  19.1 us
    all_to_all x1, blocking collectives, on_device(): exchange = lambda x: lax.all_to_all(x, 'row', 0, 0, tiled=True)  18.4 us
    pallas_call x1, Pallas kernels, cross(): pl.pallas_call(cross_kernel, grid=(2, tiles), out_shape=(pltpu.HBM((ROWS,...  15.2 us
    ppermute x7, waiting for transfers between devices, shift(): return lax.ppermute(x, 'y', [(y, (y + by) % Y) for y in range(Y)])  10.2 us
    all_to_all x1, waiting for transfers between devices, on_device(): exchange = lambda x: lax.all_to_all(x, 'row', 0, 0, tiled=True)  8.1 us
    pallas_call x1, Pallas kernels, finish(): pl.pallas_call(finish_kernel, out_shape=(pltpu.HBM((ROWS, OUT), jnp.float...  7.94 us
    ppermute x7, starting transfers between devices, shift(): return lax.ppermute(x, 'y', [(y, (y + by) % Y) for y in range(Y)])  7.4 us
    ppermute x3, starting transfers between devices, on_device(): swap = lambda x: lax.ppermute(x, 'core', [(0, 1), (1, 0)])  6.1 us
  transfers between devices with their start and end apart: 12, of which 3 were waited for; matrix products, arithmetic and copies ran while one was open for 0% of the time, Pallas kernels for 36%

profile of v2, /device:TPU:1, one launch (start us, length us, event | category | flops | bytes accessed | tf_op | source)
XLA Modules:
  0.0 114.7 jit_solution(2550283765977657212)
XLA Ops:
  0.6 0.0 copy-start.4
  0.6 0.0 copy-start.1
  0.7 0.0 copy-start
  0.7 0.0 copy-start.3
  0.7 1.5 %collective-permute-start.4 = (bf16[2048,512]{1,0:T(8,128)(2,1)}, bf16[2048,512]{1,0:T(8,128)(2,1)S(1)}, u32[]{:S(2)}, u32[]{:S(2)}) collective-permute-start(bf16[2048,512]{1,0:T(8,128)(2,1)} %refs_1_.5), channel_id=1, source_target_pairs={{0,1},{1,0},{2,3},{3,2},{4,5},{5,4},{6,7},{7,6},{8,9},{9,8},{10,11... | collective-permute-start | bytes 6291464 | tf_op jit(solution)/shard_map/ppermute | solution.py:486
  2.2 3.2 %pick.1 = bf16[16,32,512]{2,1,0:T(8,128)(2,1)} custom-call(s32[2,2048]{1,0:T(2,128)} %idx.7, bf16[2048,512]{1,0:T(8,128)(2,1)} %refs_1_.5), custom_call_target="tpu_custom_call" | custom-call | tf_op jit(solution)/shard_map/pick/pallas_call | solution.py:93
  5.4 0.0 copy-done.4
  5.4 0.0 copy-done.1
  5.5 0.0 copy-start.7
  5.5 0.0 copy-start.2
  5.5 2.9 %prepare.1 = (bf16[2048,256]{1,0:T(8,128)(2,1)}, f32[32,128]{1,0:T(8,128)S(1)}) custom-call(s32[2,2048]{1,0:T(2,128)S(1)} %copy-done.4, bf16[2048,128]{1,0:T(8,128)(2,1)S(1)} %copy-done.3, f32[2048,128]{1,0:T(8,128)S(1)} %copy-done, f32[2048,128]{1,0:T(8,128)S(1)} %copy-done.1), custom_call_target="tpu_custom_call" | custom-call | tf_op jit(solution)/shard_map/prepare/pallas_call | solution.py:127
  8.4 0.2 collective-permute-start.5
  8.6 18.4 %all_to_all.15.refs_0_.refs_8_ = bf16[16,32,512]{2,1,0:T(8,128)(2,1)S(1)} all-to-all(bf16[16,32,512]{2,1,0:T(8,128)(2,1)S(1)} %copy-done.7), channel_id=1, replica_groups=mesh['row'=16,'y'=4,'core'=2] {'row'}, dimensions={0} | all-to-all | bytes 1048576 | tf_op jit(solution)/shard_map/all_to_all | solution.py:487
  26.9 1.3 %collective-permute-start = (bf16[16,32,512]{2,1,0:T(8,128)(2,1)S(1)}, bf16[16,32,512]{2,1,0:T(8,128)(2,1)S(1)}, u32[]{:S(2)}, u32[]{:S(2)}) collective-permute-start(bf16[16,32,512]{2,1,0:T(8,128)(2,1)S(1)} %all_to_all.15.refs_0_.refs_8_), channel_id=1, source_target_pairs={{0,2},{2,4},{4,6},{6,0},{1,3},{3,5},{5,7},{7,1},{8,10},{10,12},{12... | collective-permute-start | bytes 1572872 | tf_op jit(solution)/shard_map/ppermute | solution.py:490
  28.2 1.4 %collective-permute-start.2 = (bf16[16,32,512]{2,1,0:T(8,128)(2,1)S(1)}, bf16[16,32,512]{2,1,0:T(8,128)(2,1)S(1)}, u32[]{:S(2)}, u32[]{:S(2)}) collective-permute-start(bf16[16,32,512]{2,1,0:T(8,128)(2,1)S(1)} %all_to_all.15.refs_0_.refs_8_), channel_id=1, source_target_pairs={{0,6},{2,0},{4,2},{6,4},{1,7},{3,1},{5,3},{7,5},{8,14},{10,8},{12,... | collective-permute-start | bytes 1572872 | tf_op jit(solution)/shard_map/ppermute | solution.py:490
  29.6 10.2 %collective-permute-done.refs_0_.refs_9_ = bf16[16,32,512]{2,1,0:T(8,128)(2,1)S(1)} collective-permute-done((bf16[16,32,512]{2,1,0:T(8,128)(2,1)S(1)}, bf16[16,32,512]{2,1,0:T(8,128)(2,1)S(1)}, u32[]{:S(2)}, u32[]{:S(2)}) %collective-permute-start) | collective-permute-done | bytes 524320 | tf_op jit(solution)/shard_map/ppermute | solution.py:490
  39.9 0.1 collective-permute-start.1
  40.0 0.0 collective-permute-done.2.refs_0_.refs_10_
  40.0 2.7 %collective-permute-start.3 = (bf16[8,32,512]{2,1,0:T(8,128)(2,1)S(1)}, bf16[8,32,512]{2,1,0:T(8,128)(2,1)S(1)}, u32[]{:S(2)}, u32[]{:S(2)}) collective-permute-start(bf16[8,32,512]{2,1,0:T(8,128)(2,1)S(1)} %slice.9), channel_id=1, source_target_pairs={{0,6},{2,0},{4,2},{6,4},{1,7},{3,1},{5,3},{7,5},{8,14},{10,8},{12,... | collective-permute-start | bytes 786440 | tf_op jit(solution)/shard_map/ppermute | solution.py:490
  42.7 0.0 collective-permute-done.5.refs_4_.refs_5_
  42.7 0.0 collective-permute-done.4.refs_2_.refs_3_
  42.7 4.9 %products.4 = (bf16[16,32,128]{2,1,0:T(8,128)(2,1)}, f32[2,2048]{1,0:T(2,128)S(1)}) custom-call(bf16[16,32,512]{2,1,0:T(8,128)(2,1)S(1)} %collective-permute-done.refs_0_.refs_9_, bf16[2048,512]{1,0:T(8,128)(2,1)S(1)} %copy-done.2, bf16[2048,512]{1,0:T(8,128)(2,1)S(1)} %collective-permute-done.4.refs_2_.refs_3_, bf16[2048,256]{1,0:T(8,128)(2,1)S(1)} %copy-done.6, ...), custom_call_target="tpu_custom_call" | custom-call | flops 3221225472 | bytes 1048576 | tf_op jit(solution)/shard_map/products/pallas_call | solution.py:217
  47.6 0.2 collective-permute-start.6
  47.8 4.3 %products.5 = bf16[16,32,128]{2,1,0:T(8,128)(2,1)} custom-call(bf16[16,32,512]{2,1,0:T(8,128)(2,1)S(1)} %collective-permute-done.2.refs_0_.refs_10_, bf16[2048,512]{1,0:T(8,128)(2,1)S(1)} %copy-done.2, bf16[2048,512]{1,0:T(8,128)(2,1)S(1)} %collective-permute-done.4.refs_2_.refs_3_, bf16[2048,256]{1,0:T(8,128)(2,1)S(1)} %copy-done.6, ...), custom_call_target="tpu_custom_call" | custom-call | flops 3221225472 | bytes 1048576 | tf_op jit(solution)/shard_map/products/pallas_call | solution.py:217
  52.2 1.3 %collective-permute-start.7 = (bf16[16,32,128]{2,1,0:T(8,128)(2,1)}, bf16[16,32,128]{2,1,0:T(8,128)(2,1)S(1)}, u32[]{:S(2)}, u32[]{:S(2)}) collective-permute-start(bf16[16,32,128]{2,1,0:T(8,128)(2,1)} %products.5), channel_id=1, source_target_pairs={{0,2},{2,4},{4,6},{6,0},{1,3},{3,5},{5,7},{7,1},{8,10},{10,12},{12... | collective-permute-start | bytes 393224 | tf_op jit(solution)/shard_map/ppermute | solution.py:490
  53.4 0.0 collective-permute-done.1.refs_0_.refs_11_
  53.4 0.0 collective-permute-done.3.refs_1_.refs_12_
  53.4 4.3 %products.6 = bf16[16,32,128]{2,1,0:T(8,128)(2,1)} custom-call(bf16[8,32,512]{2,1,0:T(8,128)(2,1)S(1)} %collective-permute-done.1.refs_0_.refs_11_, bf16[8,32,512]{2,1,0:T(8,128)(2,1)S(1)} %collective-permute-done.3.refs_1_.refs_12_, bf16[2048,512]{1,0:T(8,128)(2,1)S(1)} %copy-done.2, bf16[2048,512]{1,0:T(8,128)(2,1)S(1)} %collective-permute-done.4.refs_2_.refs_3_, ...), custom_call_target="tpu_custom_call" | custom-call | flops 3221225472 | bytes 1048576 | tf_op jit(solution)/shard_map/products/pallas_call | solution.py:217
  57.8 0.4 collective-permute-start.8
  58.2 0.0 collective-permute-done.7.refs_7_
  58.2 0.0 collective-permute-done.6.refs_6_
  58.2 5.6 %products.7 = (f32[16,32,128]{2,1,0:T(8,128)S(1)}, bf16[4,16,32,512]{3,2,1,0:T(8,128)(2,1)}) custom-call(bf16[16,32,512]{2,1,0:T(8,128)(2,1)S(1)} %all_to_all.15.refs_0_.refs_8_, bf16[2048,512]{1,0:T(8,128)(2,1)S(1)} %copy-done.2, bf16[2048,512]{1,0:T(8,128)(2,1)S(1)} %collective-permute-done.4.refs_2_.refs_3_, bf16[2048,256]{1,0:T(8,128)(2,1)S(1)} %copy-done.6, ...), custom_call_target="tpu_custom_call" | custom-call | flops 3221225472 | bytes 1048576 | tf_op jit(solution)/shard_map/products/pallas_call | solution.py:217
  63.8 0.0 collective-permute-done.8
  63.8 0.7 convert_add_fusion
  64.6 4.4 %collective-permute-start.9 = (bf16[64,2,16,512]{3,2,1,0:T(8,128)(2,1)}, bf16[64,2,16,512]{3,2,1,0:T(8,128)(2,1)}, u32[]{:S(2)}, u32[]{:S(2)}) collective-permute-start(bf16[64,2,16,512]{3,2,1,0:T(8,128)(2,1)} %bitcast.14), channel_id=1, source_target_pairs={{0,1},{1,0},{2,3},{3,2},{4,5},{5,4},{6,7},{7,6},{8,9},{9,8},{10,11... | collective-permute-start | bytes 6291464 | tf_op jit(solution)/shard_map/ppermute | solution.py:486
  69.0 3.5 %all-to-all-start.1 = ((f32[16,32,128]{2,1,0:T(8,128)}), f32[16,32,128]{2,1,0:T(8,128)S(1)}, u32[]{:S(2)}, u32[]{:S(2)}) async-start(f32[16,32,128]{2,1,0:T(8,128)} %convert_add_fusion), calls=%async_computation.1 | async-start | bytes 524288 | tf_op jit(solution)/shard_map/all_to_all | solution.py:487
  72.5 0.2 convert_element_type.11
  72.8 0.1 constant_dynamic-slice_fusion.1
  72.9 8.1 %all-to-all-done.1.received = f32[16,32,128]{2,1,0:T(8,128)S(1)} async-done(((f32[16,32,128]{2,1,0:T(8,128)}), f32[16,32,128]{2,1,0:T(8,128)S(1)}, u32[]{:S(2)}, u32[]{:S(2)}) %all-to-all-start.1) | async-done | bytes 262176 | tf_op jit(solution)/shard_map/all_to_all | solution.py:487
  81.0 1.1 collect.1
  82.1 5.6 %all-to-all-start.2 = ((bf16[128,32,128]{2,1,0:T(8,128)(2,1)}), bf16[128,32,128]{2,1,0:T(8,128)(2,1)S(1)}, u32[]{:S(2)}, u32[]{:S(2)}) async-start(bf16[128,32,128]{2,1,0:T(8,128)(2,1)} %get-tuple-element.35), calls=%async_computation.2 | async-start | bytes 2097152 | tf_op jit(solution)/shard_map/all_to_all | solution.py:527
  87.7 0.1 reshape.21.idx_ref
  87.8 0.0 collective-permute-done.9.other0.other1
  87.8 0.0 copy-start.5
  87.8 15.2 %cross.1 = (bf16[2048,512]{1,0:T(8,128)(2,1)}, bf16[16,2048]{1,0:T(8,128)(2,1)S(1)}) custom-call(s32[2,2048]{1,0:T(2,128)S(1)} %copy-done.4, f32[2,2,2,512]{3,2,1,0:T(2,128)S(1)} %reshape.21.idx_ref, bf16[64,2,16,512]{3,2,1,0:T(8,128)(2,1)} %bitcast.15, bf16[64,2,16,512]{3,2,1,0:T(8,128)(2,1)} %collective-permute-done.9.other0.other1, ...), custom_call_target="tpu_custom_call" | custom-call | flops 8589934592 | bytes 8388608 | tf_op jit(solution)/shard_map/cross/pallas_call | solution.py:306
  103.1 3.5 %all-to-all-done.2 = bf16[128,32,128]{2,1,0:T(8,128)(2,1)S(1)} async-done(((bf16[128,32,128]{2,1,0:T(8,128)(2,1)}), bf16[128,32,128]{2,1,0:T(8,128)(2,1)S(1)}, u32[]{:S(2)}, u32[]{:S(2)}) %all-to-all-start.2) | async-done | bytes 1048608 | tf_op jit(solution)/shard_map/all_to_all | solution.py:527
  106.5 0.0 copy-done.5
  106.5 7.9 %finish.1 = (f32[2048,128]{1,0:T(8,128)}, f32[2048,128]{1,0:T(8,128)}) custom-call(s32[2,2048]{1,0:T(2,128)S(1)} %copy-done.4, bf16[16,4,2,32,128]{4,3,2,1,0:T(8,128)(2,1)S(1)} %bitcast.11, f32[32,128]{1,0:T(8,128)S(1)} %get-tuple-element.36.after.own_grad, bf16[16,2048]{1,0:T(8,128)(2,1)S(1)} %get-tuple-element.38.own_cross, f32[2,512]{1,0:T(2,128)S(1)} %copy-done.5, ...), custom_call_target="tpu_custom_call" | custom-call | tf_op jit(solution)/shard_map/finish/pallas_call | solution.py:466
  (11 shorter events, 0.1 us)
Async XLA Ops:
  0.6 4.8 %copy-start.4 = (s32[2,2048]{1,0:T(2,128)S(1)}, s32[2,2048]{1,0:T(2,128)}, u32[]{:S(2)}) copy-start(s32[2,2048]{1,0:T(2,128)} %idx.7) | copy-start | bytes 49156
  0.6 4.8 %copy-start.1 = (f32[2048,128]{1,0:T(8,128)S(1)}, f32[2048,128]{1,0:T(8,128)}, u32[]{:S(2)}) copy-start(f32[2048,128]{1,0:T(8,128)} %aux.1) | copy-start | bytes 3145732
  0.7 4.8 %copy-start = (f32[2048,128]{1,0:T(8,128)S(1)}, f32[2048,128]{1,0:T(8,128)}, u32[]{:S(2)}) copy-start(f32[2048,128]{1,0:T(8,128)} %pri.1) | copy-start | bytes 3145732
  0.7 4.8 %copy-start.3 = (bf16[2048,128]{1,0:T(8,128)(2,1)S(1)}, bf16[2048,128]{1,0:T(8,128)(2,1)}, u32[]{:S(2)}) copy-start(bf16[2048,128]{1,0:T(8,128)(2,1)} %tgt.1) | copy-start | bytes 1572868
  0.7 42.0 %collective-permute-start.4 = (bf16[2048,512]{1,0:T(8,128)(2,1)}, bf16[2048,512]{1,0:T(8,128)(2,1)S(1)}, u32[]{:S(2)}, u32[]{:S(2)}) collective-permute-start(bf16[2048,512]{1,0:T(8,128)(2,1)} %refs_1_.5), channel_id=1, source_target_pairs={{0,1},{1,0},{2,3},{3,2},{4,5},{5,4},{6,7},{7,6},{8,9},{9,8},{10,11... | collective-permute-start | bytes 6291464 | tf_op jit(solution)/shard_map/ppermute | solution.py:486
  5.5 3.1 %copy-start.7 = (bf16[16,32,512]{2,1,0:T(8,128)(2,1)S(1)}, bf16[16,32,512]{2,1,0:T(8,128)(2,1)}, u32[]{:S(2)}) copy-start(bf16[16,32,512]{2,1,0:T(8,128)(2,1)} %pick.1) | copy-start | bytes 1572868
  5.5 37.2 %copy-start.2 = (bf16[2048,512]{1,0:T(8,128)(2,1)S(1)}, bf16[2048,512]{1,0:T(8,128)(2,1)}, u32[]{:S(2)}) copy-start(bf16[2048,512]{1,0:T(8,128)(2,1)} %refs_1_.5) | copy-start | bytes 6291460
  8.4 34.3 %copy-start.6 = (bf16[2048,256]{1,0:T(8,128)(2,1)S(1)}, bf16[2048,256]{1,0:T(8,128)(2,1)}, u32[]{:S(2)}) copy-start(bf16[2048,256]{1,0:T(8,128)(2,1)} %get-tuple-element.24.refs_3_.refs_4_) | copy-start | bytes 3145732
  8.4 34.3 %collective-permute-start.5 = (bf16[2048,256]{1,0:T(8,128)(2,1)}, bf16[2048,256]{1,0:T(8,128)(2,1)S(1)}, u32[]{:S(2)}, u32[]{:S(2)}) collective-permute-start(bf16[2048,256]{1,0:T(8,128)(2,1)} %get-tuple-element.24.refs_3_.refs_4_), channel_id=1, source_target_pairs={{0,1},{1,0},{2,3},{3,2},{4,5},{5,4},{6,7},{7,6},{8,9},{9,8},{10,11... | collective-permute-start | bytes 3145736 | tf_op jit(solution)/shard_map/ppermute | solution.py:486
  26.9 12.9 %collective-permute-start = (bf16[16,32,512]{2,1,0:T(8,128)(2,1)S(1)}, bf16[16,32,512]{2,1,0:T(8,128)(2,1)S(1)}, u32[]{:S(2)}, u32[]{:S(2)}) collective-permute-start(bf16[16,32,512]{2,1,0:T(8,128)(2,1)S(1)} %all_to_all.15.refs_0_.refs_8_), channel_id=1, source_target_pairs={{0,2},{2,4},{4,6},{6,0},{1,3},{3,5},{5,7},{7,1},{8,10},{10,12},{12... | collective-permute-start | bytes 1572872 | tf_op jit(solution)/shard_map/ppermute | solution.py:490
  28.2 11.8 %collective-permute-start.2 = (bf16[16,32,512]{2,1,0:T(8,128)(2,1)S(1)}, bf16[16,32,512]{2,1,0:T(8,128)(2,1)S(1)}, u32[]{:S(2)}, u32[]{:S(2)}) collective-permute-start(bf16[16,32,512]{2,1,0:T(8,128)(2,1)S(1)} %all_to_all.15.refs_0_.refs_8_), channel_id=1, source_target_pairs={{0,6},{2,0},{4,2},{6,4},{1,7},{3,1},{5,3},{7,5},{8,14},{10,8},{12,... | collective-permute-start | bytes 1572872 | tf_op jit(solution)/shard_map/ppermute | solution.py:490
  39.9 13.6 %collective-permute-start.1 = (bf16[8,32,512]{2,1,0:T(8,128)(2,1)S(1)}, bf16[8,32,512]{2,1,0:T(8,128)(2,1)S(1)}, u32[]{:S(2)}, u32[]{:S(2)}) collective-permute-start(bf16[8,32,512]{2,1,0:T(8,128)(2,1)S(1)} %slice.8), channel_id=1, source_target_pairs={{0,2},{2,4},{4,6},{6,0},{1,3},{3,5},{5,7},{7,1},{8,10},{10,12},{12... | collective-permute-start | bytes 786440 | tf_op jit(solution)/shard_map/ppermute | solution.py:490
  40.0 13.4 %collective-permute-start.3 = (bf16[8,32,512]{2,1,0:T(8,128)(2,1)S(1)}, bf16[8,32,512]{2,1,0:T(8,128)(2,1)S(1)}, u32[]{:S(2)}, u32[]{:S(2)}) collective-permute-start(bf16[8,32,512]{2,1,0:T(8,128)(2,1)S(1)} %slice.9), channel_id=1, source_target_pairs={{0,6},{2,0},{4,2},{6,4},{1,7},{3,1},{5,3},{7,5},{8,14},{10,8},{12,... | collective-permute-start | bytes 786440 | tf_op jit(solution)/shard_map/ppermute | solution.py:490
  47.6 10.6 %collective-permute-start.6 = (bf16[16,32,128]{2,1,0:T(8,128)(2,1)}, bf16[16,32,128]{2,1,0:T(8,128)(2,1)S(1)}, u32[]{:S(2)}, u32[]{:S(2)}) collective-permute-start(bf16[16,32,128]{2,1,0:T(8,128)(2,1)} %get-tuple-element.25), channel_id=1, source_target_pairs={{0,6},{2,0},{4,2},{6,4},{1,7},{3,1},{5,3},{7,5},{8,14},{10,8},{12,... | collective-permute-start | bytes 393224 | tf_op jit(solution)/shard_map/ppermute | solution.py:490
  52.2 6.1 %collective-permute-start.7 = (bf16[16,32,128]{2,1,0:T(8,128)(2,1)}, bf16[16,32,128]{2,1,0:T(8,128)(2,1)S(1)}, u32[]{:S(2)}, u32[]{:S(2)}) collective-permute-start(bf16[16,32,128]{2,1,0:T(8,128)(2,1)} %products.5), channel_id=1, source_target_pairs={{0,2},{2,4},{4,6},{6,0},{1,3},{3,5},{5,7},{7,1},{8,10},{10,12},{12... | collective-permute-start | bytes 393224 | tf_op jit(solution)/shard_map/ppermute | solution.py:490
  57.8 6.0 %collective-permute-start.8 = (bf16[16,32,128]{2,1,0:T(8,128)(2,1)}, bf16[16,32,128]{2,1,0:T(8,128)(2,1)S(1)}, u32[]{:S(2)}, u32[]{:S(2)}) collective-permute-start(bf16[16,32,128]{2,1,0:T(8,128)(2,1)} %products.6), channel_id=1, source_target_pairs={{0,4},{2,6},{4,0},{6,2},{1,5},{3,7},{5,1},{7,3},{8,12},{10,14},{12... | collective-permute-start | bytes 393224 | tf_op jit(solution)/shard_map/ppermute | solution.py:490
  64.6 23.2 %collective-permute-start.9 = (bf16[64,2,16,512]{3,2,1,0:T(8,128)(2,1)}, bf16[64,2,16,512]{3,2,1,0:T(8,128)(2,1)}, u32[]{:S(2)}, u32[]{:S(2)}) collective-permute-start(bf16[64,2,16,512]{3,2,1,0:T(8,128)(2,1)} %bitcast.14), channel_id=1, source_target_pairs={{0,1},{1,0},{2,3},{3,2},{4,5},{5,4},{6,7},{7,6},{8,9},{9,8},{10,11... | collective-permute-start | bytes 6291464 | tf_op jit(solution)/shard_map/ppermute | solution.py:486
  69.0 12.0 %all-to-all-start.1 = ((f32[16,32,128]{2,1,0:T(8,128)}), f32[16,32,128]{2,1,0:T(8,128)S(1)}, u32[]{:S(2)}, u32[]{:S(2)}) async-start(f32[16,32,128]{2,1,0:T(8,128)} %convert_add_fusion), calls=%async_computation.1 | async-start | bytes 524288 | tf_op jit(solution)/shard_map/all_to_all | solution.py:487
  82.1 24.5 %all-to-all-start.2 = ((bf16[128,32,128]{2,1,0:T(8,128)(2,1)}), bf16[128,32,128]{2,1,0:T(8,128)(2,1)S(1)}, u32[]{:S(2)}, u32[]{:S(2)}) async-start(bf16[128,32,128]{2,1,0:T(8,128)(2,1)} %get-tuple-element.35), calls=%async_computation.2 | async-start | bytes 2097152 | tf_op jit(solution)/shard_map/all_to_all | solution.py:527
  87.8 18.7 %copy-start.5 = (f32[2,512]{1,0:T(2,128)S(1)}, f32[2,512]{1,0:T(2,128)}, u32[]{:S(2)}) copy-start(f32[2,512]{1,0:T(2,128)} %spectrum.1) | copy-start | bytes 12292

commit v3 on v2

--- a/solution.py
+++ b/solution.py
@@ -106,10 +106,11 @@
     )(indices, features)
 
 
-def prepare_kernel(idx, tgt, pri, aux, blend_bf, extra):
-    blend0, _, blend1 = blends(aux[...], pri[...])
-    blend_bf[:, :OUT] = blend0.astype(jnp.bfloat16)
-    blend_bf[:, OUT:] = blend1.astype(jnp.bfloat16)
+def prepare_kernel(idx, tgt, pri, aux, other_pri, other_aux, blend_bf, other_blend, extra):
+    for a, p, out in ((aux, pri, blend_bf), (other_aux, other_pri, other_blend)):
+        blend0, _, blend1 = blends(a[...], p[...])
+        out[:, :OUT] = blend0.astype(jnp.bfloat16)
+        out[:, OUT:] = blend1.astype(jnp.bfloat16)
     which = lax.broadcasted_iota(jnp.int32, (STEPS * OWN, 1), 0)
     column = jnp.zeros((STEPS * OWN, 1), jnp.int32)
     for at in range(STEPS * OWN):
@@ -122,19 +123,20 @@
     extra[...] -= jnp.dot(chosen, tgt[...], preferred_element_type=jnp.float32)
 
 
-def prepare(indices, targets, primary, auxiliary):
+def prepare(indices, targets, *weights):
     vmem = pl.BlockSpec(memory_space=pltpu.VMEM)
     return pl.pallas_call(
         prepare_kernel,
         out_shape=(
-            pltpu.HBM((ROWS, STEPS * OUT), jnp.bfloat16),
+            jax.ShapeDtypeStruct((ROWS, STEPS * OUT), jnp.bfloat16),
+            jax.ShapeDtypeStruct((ROWS, STEPS * OUT), jnp.bfloat16),
             jax.ShapeDtypeStruct((STEPS * OWN, OUT), jnp.float32),
         ),
-        in_specs=[pl.BlockSpec(memory_space=pltpu.SMEM)] + [vmem] * 3,
-        out_specs=(vmem,) * 2,
+        in_specs=[pl.BlockSpec(memory_space=pltpu.SMEM)] + [vmem] * 5,
+        out_specs=(vmem,) * 3,
         compiler_params=pltpu.CompilerParams(vmem_limit_bytes=16 * MIB),
         name="prepare",
-    )(indices, targets, primary, auxiliary)
+    )(indices, targets, *weights)
 
 
 SCALE = LOG2E / (2.0 * D)
@@ -333,7 +335,7 @@
 
 
 def collect_kernel(received, extra, own_grad, send):
-    total = jnp.sum(received[...], axis=0) + extra[...]
+    total = jnp.sum(received[...].astype(jnp.float32), axis=0) + extra[...]
     own_grad[...] = total
     send[...] = jnp.broadcast_to(total.astype(jnp.bfloat16)[None], send.shape)
 
@@ -489,19 +491,20 @@
     def shift(x, by):
         return lax.ppermute(x, "y", [(y, (y + by) % Y) for y in range(Y)])
 
-    send = pick(indices, features)
-    other_features = swap(features)
-    send, primary, auxiliary = lax.optimization_barrier((send, primary, auxiliary))
-    here = exchange(send)
-    blend_bf, extra = prepare(indices, targets, primary, auxiliary)
-    blend_bf = (blend_bf, swap(blend_bf))
+    send, own = lax.optimization_barrier((pick(indices, features), (features, primary, auxiliary)))
+    other_features, other_primary, other_auxiliary = [swap(x) for x in own]
     features = (features, other_features)
     by_core = indices.reshape(STEPS, LINE, Y, 2, OWN).astype(jnp.float32)
     halves = [lax.dynamic_index_in_dim(by_core, at, 3, False) for at in (core, 1 - core)]
     idx_halves = jnp.stack(halves).transpose(0, 1, 3, 2, 4).reshape(2, STEPS, CHIPS // WIDE, WIDE * OWN)
 
+    here = exchange(send)
     below = shift(here, 1)
     above = shift(here, -1)
+    weights = (primary, auxiliary, other_primary, other_auxiliary)
+    _, weights = lax.optimization_barrier((here, weights))
+    *blend_bf, extra = prepare(indices, targets, *weights)
+    below, above, blend_bf = lax.optimization_barrier((below, above, blend_bf))
     across = (shift(below[: LINE // 2], 1), shift(above[LINE // 2:], -1))
     to_below, norms = products((below,), features, blend_bf)
     norms = (norms,)
@@ -516,7 +519,7 @@
     partial, block = products(
         (here_late,), features, blend_bf, norms, (for_below, for_above), (here, below, above) + across
     )
-    partial = partial + for_across.astype(jnp.float32)
+    partial = (partial + for_across.astype(jnp.float32)).astype(jnp.bfloat16)
     block, partial = lax.optimization_barrier((block, partial))
     block = block.reshape(CHIPS, STEPS, OWN, D)
     other_block = swap(block)

time: 115 us -> 113 us (0.983)
  waiting for transfers between devices: 21.8 us -> 18.3 us
    ppermute x7, waiting for transfers between devices: 10.2 us -> 7.78 us  [shift(): return lax.ppermute(x, 'y', [(y, (y + by) % Y) for y in range(Y)])]
    ppermute x3 -> x4, starting transfers between devices: 6.1 us -> 7.55 us  [on_device(): swap = lambda x: lax.ppermute(x, 'core', [(0, 1), (1, 0)])]
    all_to_all x1, starting transfers between devices: 5.57 us -> 4.34 us  [on_device(): lax.all_to_all(tosend, ALL, 0, 0, tiled=True)]
    all_to_all x1, waiting for transfers between devices: 8.1 us -> 6.9 us  [on_device(): exchange = lambda x: lax.all_to_all(x, 'row', 0, 0, tiled=True)]
  transfers between devices with their start and end apart: 12 -> 13, of which waited for: 3 -> 3; matrix products, arithmetic and copies ran while one was open for 0% -> 0% of each run, Pallas kernels for 36% -> 34%
where the time goes in v3:
time: 113 us; the launch traced here: 112 us
  Pallas kernels  49.6 us (44%)
  starting transfers between devices  23.5 us (21%)
  blocking collectives  18.7 us (17%)
  waiting for transfers between devices  18.3 us (16%)
    pallas_call x4, Pallas kernels, products(): pl.pallas_call(functools.partial(product_kernel, pieces=len(pieces), sums...  19.1 us
    all_to_all x1, blocking collectives, on_device(): exchange = lambda x: lax.all_to_all(x, 'row', 0, 0, tiled=True)  18.7 us
    pallas_call x1, Pallas kernels, cross(): pl.pallas_call(cross_kernel, grid=(2, tiles), out_shape=(pltpu.HBM((ROWS,...  15.2 us
    ppermute x7, starting transfers between devices, shift(): return lax.ppermute(x, 'y', [(y, (y + by) % Y) for y in range(Y)])  8.1 us
    pallas_call x1, Pallas kernels, finish(): pl.pallas_call(finish_kernel, out_shape=(pltpu.HBM((ROWS, OUT), jnp.float...  7.94 us
    ppermute x7, waiting for transfers between devices, shift(): return lax.ppermute(x, 'y', [(y, (y + by) % Y) for y in range(Y)])  7.78 us
    ppermute x4, starting transfers between devices, on_device(): swap = lambda x: lax.ppermute(x, 'core', [(0, 1), (1, 0)])  7.55 us
    all_to_all x1, waiting for transfers between devices, on_device(): exchange = lambda x: lax.all_to_all(x, 'row', 0, 0, tiled=True)  6.9 us
  transfers between devices with their start and end apart: 13, of which 3 were waited for; matrix products, arithmetic and copies ran while one was open for 0% of the time, Pallas kernels for 34%

profile of v3, /device:TPU:1, one launch (start us, length us, event | category | flops | bytes accessed | tf_op | source)
XLA Modules:
  0.0 112.3 jit_solution(2661372512936505950)
XLA Ops:
  0.6 0.0 copy-start.4
  0.6 0.0 copy-start.1
  0.7 0.0 copy-start
  0.7 0.0 copy-start.3
  0.7 3.5 %pick.1 = bf16[16,32,512]{2,1,0:T(8,128)(2,1)} custom-call(s32[2,2048]{1,0:T(2,128)} %idx.7, bf16[2048,512]{1,0:T(8,128)(2,1)} %refs_1_.5), custom_call_target="tpu_custom_call" | custom-call | tf_op jit(solution)/shard_map/pick/pallas_call | solution.py:93
  4.1 1.5 %collective-permute-start.6 = (bf16[2048,512]{1,0:T(8,128)(2,1)}, bf16[2048,512]{1,0:T(8,128)(2,1)S(1)}, u32[]{:S(2)}, u32[]{:S(2)}) collective-permute-start(bf16[2048,512]{1,0:T(8,128)(2,1)} %refs_1_.5), channel_id=1, source_target_pairs={{0,1},{1,0},{2,3},{3,2},{4,5},{5,4},{6,7},{7,6},{8,9},{9,8},{10,11... | collective-permute-start | bytes 6291464 | tf_op jit(solution)/shard_map/ppermute | solution.py:488
  5.6 0.1 collective-permute-start.2
  5.7 0.0 copy-done.1
  5.7 0.4 collective-permute-start.3
  6.1 18.7 %all_to_all.15.refs_0_.refs_8_ = bf16[16,32,512]{2,1,0:T(8,128)(2,1)S(1)} all-to-all(bf16[16,32,512]{2,1,0:T(8,128)(2,1)} %pick.1), channel_id=1, replica_groups=mesh['row'=16,'y'=4,'core'=2] {'row'}, dimensions={0} | all-to-all | bytes 1048576 | tf_op jit(solution)/shard_map/all_to_all | solution.py:489
  24.8 1.3 %collective-permute-start = (bf16[16,32,512]{2,1,0:T(8,128)(2,1)S(1)}, bf16[16,32,512]{2,1,0:T(8,128)(2,1)S(1)}, u32[]{:S(2)}, u32[]{:S(2)}) collective-permute-start(bf16[16,32,512]{2,1,0:T(8,128)(2,1)S(1)} %all_to_all.15.refs_0_.refs_8_), channel_id=1, source_target_pairs={{0,2},{2,4},{4,6},{6,0},{1,3},{3,5},{5,7},{7,1},{8,10},{10,12},{12... | collective-permute-start | bytes 1572872 | tf_op jit(solution)/shard_map/ppermute | solution.py:492
  26.1 1.4 %collective-permute-start.1 = (bf16[16,32,512]{2,1,0:T(8,128)(2,1)S(1)}, bf16[16,32,512]{2,1,0:T(8,128)(2,1)S(1)}, u32[]{:S(2)}, u32[]{:S(2)}) collective-permute-start(bf16[16,32,512]{2,1,0:T(8,128)(2,1)S(1)} %all_to_all.15.refs_0_.refs_8_), channel_id=1, source_target_pairs={{0,6},{2,0},{4,2},{6,4},{1,7},{3,1},{5,3},{7,5},{8,14},{10,8},{12,... | collective-permute-start | bytes 1572872 | tf_op jit(solution)/shard_map/ppermute | solution.py:492
  27.5 0.0 collective-permute-done.2.other_pri
  27.5 0.0 collective-permute-done.3.other_aux
  27.5 0.0 copy-done.4
  27.6 2.7 %prepare.1 = (bf16[2048,256]{1,0:T(8,128)(2,1)S(1)}, bf16[2048,256]{1,0:T(8,128)(2,1)S(1)}, f32[32,128]{1,0:T(8,128)S(1)}) custom-call(s32[2,2048]{1,0:T(2,128)S(1)} %copy-done.4, bf16[2048,128]{1,0:T(8,128)(2,1)S(1)} %copy-done.3, f32[2048,128]{1,0:T(8,128)S(1)} %copy-done, f32[2048,128]{1,0:T(8,128)S(1)} %copy-done.1, ...), custom_call_target="tpu_custom_call" | custom-call | tf_op jit(solution)/shard_map/prepare/pallas_call | solution.py:128
  30.3 7.8 %collective-permute-done.refs_0_.refs_9_ = bf16[16,32,512]{2,1,0:T(8,128)(2,1)S(1)} collective-permute-done((bf16[16,32,512]{2,1,0:T(8,128)(2,1)S(1)}, bf16[16,32,512]{2,1,0:T(8,128)(2,1)S(1)}, u32[]{:S(2)}, u32[]{:S(2)}) %collective-permute-start) | collective-permute-done | bytes 524320 | tf_op jit(solution)/shard_map/ppermute | solution.py:492
  38.1 0.0 collective-permute-done.1.refs_0_.refs_10_
  38.1 1.0 collective-permute-start.4
  39.2 1.8 %collective-permute-start.5 = (bf16[8,32,512]{2,1,0:T(8,128)(2,1)S(1)}, bf16[8,32,512]{2,1,0:T(8,128)(2,1)S(1)}, u32[]{:S(2)}, u32[]{:S(2)}) collective-permute-start(bf16[8,32,512]{2,1,0:T(8,128)(2,1)S(1)} %slice.7), channel_id=1, source_target_pairs={{0,6},{2,0},{4,2},{6,4},{1,7},{3,1},{5,3},{7,5},{8,14},{10,8},{12,... | collective-permute-start | bytes 786440 | tf_op jit(solution)/shard_map/ppermute | solution.py:492
  40.9 0.0 collective-permute-done.6.refs_2_.refs_3_
  40.9 0.0 copy-done.2
  40.9 4.9 %products.4 = (bf16[16,32,128]{2,1,0:T(8,128)(2,1)}, f32[2,2048]{1,0:T(2,128)S(1)}) custom-call(bf16[16,32,512]{2,1,0:T(8,128)(2,1)S(1)} %collective-permute-done.refs_0_.refs_9_, bf16[2048,512]{1,0:T(8,128)(2,1)S(1)} %copy-done.2, bf16[2048,512]{1,0:T(8,128)(2,1)S(1)} %collective-permute-done.6.refs_2_.refs_3_, ...), custom_call_target="tpu_custom_call" | custom-call | flops 3221225472 | bytes 1048576 | tf_op jit(solution)/shard_map/products/pallas_call | solution.py:219
  45.8 1.2 %collective-permute-start.7 = (bf16[16,32,128]{2,1,0:T(8,128)(2,1)}, bf16[16,32,128]{2,1,0:T(8,128)(2,1)S(1)}, u32[]{:S(2)}, u32[]{:S(2)}) collective-permute-start(bf16[16,32,128]{2,1,0:T(8,128)(2,1)} %get-tuple-element.45), channel_id=1, source_target_pairs={{0,6},{2,0},{4,2},{6,4},{1,7},{3,1},{5,3},{7,5},{8,14},{10,8},{12,... | collective-permute-start | bytes 393224 | tf_op jit(solution)/shard_map/ppermute | solution.py:492
  47.0 4.3 %products.5 = bf16[16,32,128]{2,1,0:T(8,128)(2,1)} custom-call(bf16[16,32,512]{2,1,0:T(8,128)(2,1)S(1)} %collective-permute-done.1.refs_0_.refs_10_, bf16[2048,512]{1,0:T(8,128)(2,1)S(1)} %copy-done.2, bf16[2048,512]{1,0:T(8,128)(2,1)S(1)} %collective-permute-done.6.refs_2_.refs_3_, bf16[2048,256]{1,0:T(8,128)(2,1)S(1)} %get-tuple-element.43.refs_3_.refs_4_, ...), custom_call_target="tpu_custom_call" | custom-call | flops 3221225472 | bytes 1048576 | tf_op jit(solution)/shard_map/products/pallas_call | solution.py:219
  51.3 0.3 collective-permute-start.8
  51.6 0.0 collective-permute-done.4.refs_0_.refs_11_
  51.6 0.0 collective-permute-done.5.refs_1_.refs_12_
  51.6 4.3 %products.6 = bf16[16,32,128]{2,1,0:T(8,128)(2,1)} custom-call(bf16[8,32,512]{2,1,0:T(8,128)(2,1)S(1)} %collective-permute-done.4.refs_0_.refs_11_, bf16[8,32,512]{2,1,0:T(8,128)(2,1)S(1)} %collective-permute-done.5.refs_1_.refs_12_, bf16[2048,512]{1,0:T(8,128)(2,1)S(1)} %copy-done.2, bf16[2048,512]{1,0:T(8,128)(2,1)S(1)} %collective-permute-done.6.refs_2_.refs_3_, ...), custom_call_target="tpu_custom_call" | custom-call | flops 3221225472 | bytes 1048576 | tf_op jit(solution)/shard_map/products/pallas_call | solution.py:219
  56.0 1.1 collective-permute-start.9
  57.1 0.0 collective-permute-done.8.refs_7_
  57.1 0.0 collective-permute-done.7.refs_6_
  57.1 5.6 %products.7 = (f32[16,32,128]{2,1,0:T(8,128)S(1)}, bf16[4,16,32,512]{3,2,1,0:T(8,128)(2,1)}) custom-call(bf16[16,32,512]{2,1,0:T(8,128)(2,1)S(1)} %all_to_all.15.refs_0_.refs_8_, bf16[2048,512]{1,0:T(8,128)(2,1)S(1)} %copy-done.2, bf16[2048,512]{1,0:T(8,128)(2,1)S(1)} %collective-permute-done.6.refs_2_.refs_3_, ...), custom_call_target="tpu_custom_call" | custom-call | flops 3221225472 | bytes 1048576 | tf_op jit(solution)/shard_map/products/pallas_call | solution.py:219
  62.6 0.0 collective-permute-done.9
  62.7 0.7 add_convert_fusion
  63.3 5.6 %collective-permute-start.10 = (bf16[64,2,16,512]{3,2,1,0:T(8,128)(2,1)}, bf16[64,2,16,512]{3,2,1,0:T(8,128)(2,1)}, u32[]{:S(2)}, u32[]{:S(2)}) collective-permute-start(bf16[64,2,16,512]{3,2,1,0:T(8,128)(2,1)} %bitcast.14), channel_id=1, source_target_pairs={{0,1},{1,0},{2,3},{3,2},{4,5},{5,4},{6,7},{7,6},{8,9},{9,8},{10,11... | collective-permute-start | bytes 6291464 | tf_op jit(solution)/shard_map/ppermute | solution.py:488
  68.9 3.5 %all-to-all-start.1 = ((bf16[16,32,128]{2,1,0:T(8,128)(2,1)}), bf16[16,32,128]{2,1,0:T(8,128)(2,1)S(1)}, u32[]{:S(2)}, u32[]{:S(2)}) async-start(bf16[16,32,128]{2,1,0:T(8,128)(2,1)} %add_convert_fusion), calls=%async_computation.1 | async-start | bytes 262144 | tf_op jit(solution)/shard_map/all_to_all | solution.py:489
  72.4 0.2 convert_element_type.15
  72.7 0.1 constant_dynamic-slice_fusion.1
  72.8 6.9 %all-to-all-done.1.received = bf16[16,32,128]{2,1,0:T(8,128)(2,1)S(1)} async-done(((bf16[16,32,128]{2,1,0:T(8,128)(2,1)}), bf16[16,32,128]{2,1,0:T(8,128)(2,1)S(1)}, u32[]{:S(2)}, u32[]{:S(2)}) %all-to-all-start.1) | async-done | bytes 131104 | tf_op jit(solution)/shard_map/all_to_all | solution.py:489
  79.7 1.1 collect.1
  80.8 4.3 %all-to-all-start.2 = ((bf16[128,32,128]{2,1,0:T(8,128)(2,1)}), bf16[128,32,128]{2,1,0:T(8,128)(2,1)S(1)}, u32[]{:S(2)}, u32[]{:S(2)}) async-start(bf16[128,32,128]{2,1,0:T(8,128)(2,1)} %get-tuple-element.55), calls=%async_computation.2 | async-start | bytes 2097152 | tf_op jit(solution)/shard_map/all_to_all | solution.py:530
  85.1 0.1 reshape.21.idx_ref
  85.3 0.0 collective-permute-done.10.other0.other1
  85.3 0.0 copy-start.5
  85.3 15.2 %cross.1 = (bf16[2048,512]{1,0:T(8,128)(2,1)}, bf16[16,2048]{1,0:T(8,128)(2,1)S(1)}) custom-call(s32[2,2048]{1,0:T(2,128)S(1)} %copy-done.4, f32[2,2,2,512]{3,2,1,0:T(2,128)S(1)} %reshape.21.idx_ref, bf16[64,2,16,512]{3,2,1,0:T(8,128)(2,1)} %bitcast.15, bf16[64,2,16,512]{3,2,1,0:T(8,128)(2,1)} %collective-permute-done.10.other0.other1, ...), custom_call_target="tpu_custom_call" | custom-call | flops 8589934592 | bytes 8388608 | tf_op jit(solution)/shard_map/cross/pallas_call | solution.py:308
  100.5 3.6 %all-to-all-done.2 = bf16[128,32,128]{2,1,0:T(8,128)(2,1)S(1)} async-done(((bf16[128,32,128]{2,1,0:T(8,128)(2,1)}), bf16[128,32,128]{2,1,0:T(8,128)(2,1)S(1)}, u32[]{:S(2)}, u32[]{:S(2)}) %all-to-all-start.2) | async-done | bytes 1048608 | tf_op jit(solution)/shard_map/all_to_all | solution.py:530
  104.1 7.9 %finish.1 = (f32[2048,128]{1,0:T(8,128)}, f32[2048,128]{1,0:T(8,128)}) custom-call(s32[2,2048]{1,0:T(2,128)S(1)} %copy-done.4, bf16[16,4,2,32,128]{4,3,2,1,0:T(8,128)(2,1)S(1)} %bitcast.11, f32[32,128]{1,0:T(8,128)S(1)} %get-tuple-element.56.after.own_grad, bf16[16,2048]{1,0:T(8,128)(2,1)S(1)} %get-tuple-element.58.own_cross, f32[2,512]{1,0:T(2,128)S(1)} %copy-done.5, ...), custom_call_target="tpu_custom_call" | custom-call | tf_op jit(solution)/shard_map/finish/pallas_call | solution.py:468
  (9 shorter events, 0.1 us)
Async XLA Ops:
  0.6 26.9 %copy-start.4 = (s32[2,2048]{1,0:T(2,128)S(1)}, s32[2,2048]{1,0:T(2,128)}, u32[]{:S(2)}) copy-start(s32[2,2048]{1,0:T(2,128)} %idx.7) | copy-start | bytes 49156
  0.6 5.1 %copy-start.1 = (f32[2048,128]{1,0:T(8,128)S(1)}, f32[2048,128]{1,0:T(8,128)}, u32[]{:S(2)}) copy-start(f32[2048,128]{1,0:T(8,128)} %aux.2) | copy-start | bytes 3145732
  0.7 5.0 %copy-start = (f32[2048,128]{1,0:T(8,128)S(1)}, f32[2048,128]{1,0:T(8,128)}, u32[]{:S(2)}) copy-start(f32[2048,128]{1,0:T(8,128)} %pri.2) | copy-start | bytes 3145732
  0.7 26.9 %copy-start.3 = (bf16[2048,128]{1,0:T(8,128)(2,1)S(1)}, bf16[2048,128]{1,0:T(8,128)(2,1)}, u32[]{:S(2)}) copy-start(bf16[2048,128]{1,0:T(8,128)(2,1)} %tgt.1) | copy-start | bytes 1572868
  4.1 36.8 %collective-permute-start.6 = (bf16[2048,512]{1,0:T(8,128)(2,1)}, bf16[2048,512]{1,0:T(8,128)(2,1)S(1)}, u32[]{:S(2)}, u32[]{:S(2)}) collective-permute-start(bf16[2048,512]{1,0:T(8,128)(2,1)} %refs_1_.5), channel_id=1, source_target_pairs={{0,1},{1,0},{2,3},{3,2},{4,5},{5,4},{6,7},{7,6},{8,9},{9,8},{10,11... | collective-permute-start | bytes 6291464 | tf_op jit(solution)/shard_map/ppermute | solution.py:488
  5.6 21.9 %collective-permute-start.2 = (f32[2048,128]{1,0:T(8,128)S(1)}, f32[2048,128]{1,0:T(8,128)S(1)}, u32[]{:S(2)}, u32[]{:S(2)}) collective-permute-start(f32[2048,128]{1,0:T(8,128)S(1)} %copy-done), channel_id=1, source_target_pairs={{0,1},{1,0},{2,3},{3,2},{4,5},{5,4},{6,7},{7,6},{8,9},{9,8},{10,11... | collective-permute-start | bytes 3145736 | tf_op jit(solution)/shard_map/ppermute | solution.py:488
  5.7 21.8 %collective-permute-start.3 = (f32[2048,128]{1,0:T(8,128)S(1)}, f32[2048,128]{1,0:T(8,128)S(1)}, u32[]{:S(2)}, u32[]{:S(2)}) collective-permute-start(f32[2048,128]{1,0:T(8,128)S(1)} %copy-done.1), channel_id=1, source_target_pairs={{0,1},{1,0},{2,3},{3,2},{4,5},{5,4},{6,7},{7,6},{8,9},{9,8},{10,11... | collective-permute-start | bytes 3145736 | tf_op jit(solution)/shard_map/ppermute | solution.py:488
  24.8 16.1 %copy-start.2 = (bf16[2048,512]{1,0:T(8,128)(2,1)S(1)}, bf16[2048,512]{1,0:T(8,128)(2,1)}, u32[]{:S(2)}) copy-start(bf16[2048,512]{1,0:T(8,128)(2,1)} %refs_1_.5) | copy-start | bytes 6291460
  24.8 13.3 %collective-permute-start = (bf16[16,32,512]{2,1,0:T(8,128)(2,1)S(1)}, bf16[16,32,512]{2,1,0:T(8,128)(2,1)S(1)}, u32[]{:S(2)}, u32[]{:S(2)}) collective-permute-start(bf16[16,32,512]{2,1,0:T(8,128)(2,1)S(1)} %all_to_all.15.refs_0_.refs_8_), channel_id=1, source_target_pairs={{0,2},{2,4},{4,6},{6,0},{1,3},{3,5},{5,7},{7,1},{8,10},{10,12},{12... | collective-permute-start | bytes 1572872 | tf_op jit(solution)/shard_map/ppermute | solution.py:492
  26.1 12.0 %collective-permute-start.1 = (bf16[16,32,512]{2,1,0:T(8,128)(2,1)S(1)}, bf16[16,32,512]{2,1,0:T(8,128)(2,1)S(1)}, u32[]{:S(2)}, u32[]{:S(2)}) collective-permute-start(bf16[16,32,512]{2,1,0:T(8,128)(2,1)S(1)} %all_to_all.15.refs_0_.refs_8_), channel_id=1, source_target_pairs={{0,6},{2,0},{4,2},{6,4},{1,7},{3,1},{5,3},{7,5},{8,14},{10,8},{12,... | collective-permute-start | bytes 1572872 | tf_op jit(solution)/shard_map/ppermute | solution.py:492
  38.1 13.6 %collective-permute-start.4 = (bf16[8,32,512]{2,1,0:T(8,128)(2,1)S(1)}, bf16[8,32,512]{2,1,0:T(8,128)(2,1)S(1)}, u32[]{:S(2)}, u32[]{:S(2)}) collective-permute-start(bf16[8,32,512]{2,1,0:T(8,128)(2,1)S(1)} %slice.6), channel_id=1, source_target_pairs={{0,2},{2,4},{4,6},{6,0},{1,3},{3,5},{5,7},{7,1},{8,10},{10,12},{12... | collective-permute-start | bytes 786440 | tf_op jit(solution)/shard_map/ppermute | solution.py:492
  39.2 12.5 %collective-permute-start.5 = (bf16[8,32,512]{2,1,0:T(8,128)(2,1)S(1)}, bf16[8,32,512]{2,1,0:T(8,128)(2,1)S(1)}, u32[]{:S(2)}, u32[]{:S(2)}) collective-permute-start(bf16[8,32,512]{2,1,0:T(8,128)(2,1)S(1)} %slice.7), channel_id=1, source_target_pairs={{0,6},{2,0},{4,2},{6,4},{1,7},{3,1},{5,3},{7,5},{8,14},{10,8},{12,... | collective-permute-start | bytes 786440 | tf_op jit(solution)/shard_map/ppermute | solution.py:492
  45.8 11.2 %collective-permute-start.7 = (bf16[16,32,128]{2,1,0:T(8,128)(2,1)}, bf16[16,32,128]{2,1,0:T(8,128)(2,1)S(1)}, u32[]{:S(2)}, u32[]{:S(2)}) collective-permute-start(bf16[16,32,128]{2,1,0:T(8,128)(2,1)} %get-tuple-element.45), channel_id=1, source_target_pairs={{0,6},{2,0},{4,2},{6,4},{1,7},{3,1},{5,3},{7,5},{8,14},{10,8},{12,... | collective-permute-start | bytes 393224 | tf_op jit(solution)/shard_map/ppermute | solution.py:492
  51.3 5.7 %collective-permute-start.8 = (bf16[16,32,128]{2,1,0:T(8,128)(2,1)}, bf16[16,32,128]{2,1,0:T(8,128)(2,1)S(1)}, u32[]{:S(2)}, u32[]{:S(2)}) collective-permute-start(bf16[16,32,128]{2,1,0:T(8,128)(2,1)} %products.5), channel_id=1, source_target_pairs={{0,2},{2,4},{4,6},{6,0},{1,3},{3,5},{5,7},{7,1},{8,10},{10,12},{12... | collective-permute-start | bytes 393224 | tf_op jit(solution)/shard_map/ppermute | solution.py:492
  56.0 6.7 %collective-permute-start.9 = (bf16[16,32,128]{2,1,0:T(8,128)(2,1)}, bf16[16,32,128]{2,1,0:T(8,128)(2,1)S(1)}, u32[]{:S(2)}, u32[]{:S(2)}) collective-permute-start(bf16[16,32,128]{2,1,0:T(8,128)(2,1)} %products.6), channel_id=1, source_target_pairs={{0,4},{2,6},{4,0},{6,2},{1,5},{3,7},{5,1},{7,3},{8,12},{10,14},{12... | collective-permute-start | bytes 393224 | tf_op jit(solution)/shard_map/ppermute | solution.py:492
  63.3 21.9 %collective-permute-start.10 = (bf16[64,2,16,512]{3,2,1,0:T(8,128)(2,1)}, bf16[64,2,16,512]{3,2,1,0:T(8,128)(2,1)}, u32[]{:S(2)}, u32[]{:S(2)}) collective-permute-start(bf16[64,2,16,512]{3,2,1,0:T(8,128)(2,1)} %bitcast.14), channel_id=1, source_target_pairs={{0,1},{1,0},{2,3},{3,2},{4,5},{5,4},{6,7},{7,6},{8,9},{9,8},{10,11... | collective-permute-start | bytes 6291464 | tf_op jit(solution)/shard_map/ppermute | solution.py:488
  68.9 10.8 %all-to-all-start.1 = ((bf16[16,32,128]{2,1,0:T(8,128)(2,1)}), bf16[16,32,128]{2,1,0:T(8,128)(2,1)S(1)}, u32[]{:S(2)}, u32[]{:S(2)}) async-start(bf16[16,32,128]{2,1,0:T(8,128)(2,1)} %add_convert_fusion), calls=%async_computation.1 | async-start | bytes 262144 | tf_op jit(solution)/shard_map/all_to_all | solution.py:489
  80.8 23.4 %all-to-all-start.2 = ((bf16[128,32,128]{2,1,0:T(8,128)(2,1)}), bf16[128,32,128]{2,1,0:T(8,128)(2,1)S(1)}, u32[]{:S(2)}, u32[]{:S(2)}) async-start(bf16[128,32,128]{2,1,0:T(8,128)(2,1)} %get-tuple-element.55), calls=%async_computation.2 | async-start | bytes 2097152 | tf_op jit(solution)/shard_map/all_to_all | solution.py:530
  85.3 18.9 %copy-start.5 = (f32[2,512]{1,0:T(2,128)S(1)}, f32[2,512]{1,0:T(2,128)}, u32[]{:S(2)}) copy-start(f32[2,512]{1,0:T(2,128)} %spectrum.1) | copy-start | bytes 12292

commit v4 on v3

--- a/solution.py
+++ b/solution.py
@@ -281,21 +281,18 @@
                 total += jnp.dot(values, factor, preferred_element_type=jnp.float32)
             behind = ahead
         weights[...] = total.astype(jnp.bfloat16)
+        mine = own1[place(), 0]
+        which_row = lax.broadcasted_iota(jnp.int32, (OWN, 1), 0)
+        column = jnp.zeros((OWN, 1), jnp.int32)
+        position = chip_index() * 2 + core
+        for i in range(OWN):
+            column = jnp.where(which_row == i, idx[1, position * OWN + i], column)
+        kernel = kernel_values(mine, row_norms(mine), block, norm_row(block))
+        kernel += jnp.where(column.astype(jnp.float32) == here, ridge_coef, 0.0)
+        own_rows[...] = kernel.astype(jnp.bfloat16)
 
     pl.when(opening)(lambda: tile_of(True))
     pl.when(jnp.logical_not(opening))(lambda: tile_of(False))
-
-    block = jnp.where(half == 0, own0[...], other0[...]).reshape(size, D)
-    here = idx_ref[pl.ds(half, 1), 0, pl.ds(tile, 1), :].reshape(1, size)
-    mine = own1[place(), 0]
-    which_row = lax.broadcasted_iota(jnp.int32, (OWN, 1), 0)
-    column = jnp.zeros((OWN, 1), jnp.int32)
-    position = chip_index() * 2 + core
-    for i in range(OWN):
-        column = jnp.where(which_row == i, idx[1, position * OWN + i], column)
-    kernel = kernel_values(mine, row_norms(mine), block, norm_row(block))
-    kernel += jnp.where(column.astype(jnp.float32) == here, ridge_coef, 0.0)
-    own_rows[...] = kernel.astype(jnp.bfloat16)
 
 
 def cross(indices, own, other, idx, factors, after):
@@ -346,7 +343,7 @@
         collect_kernel,
         out_shape=(
             jax.ShapeDtypeStruct((STEPS * OWN, OUT), jnp.float32),
-            jax.ShapeDtypeStruct((2 * CHIPS, STEPS * OWN, OUT), jnp.bfloat16),
+            jax.ShapeDtypeStruct((CHIPS, STEPS * OWN, OUT), jnp.bfloat16),
         ),
         in_specs=[vmem, vmem],
         out_specs=(vmem, vmem),
@@ -367,7 +364,7 @@
 
 
 def finish_kernel(
-    idx, grads, own_grad, own_cross, spectrum, factors, weights, pri, aux,
+    idx, grads0, grads1, own_grad, own_cross, spectrum, factors, weights, pri, aux,
     pri_out, aux_out, result, factor_ref, weights_ref, sems, load_sems, factor_sems,
 ):
     chip = place()
@@ -392,10 +389,8 @@
         return factor_ref[step, half].reshape(count, D)
 
     def gradient(step, half):
-        other = lax.bitwise_xor(core, half)
-        wide = [
-            grads[:, y, other, step * OWN:(step + 1) * OWN, :].reshape(LINE * OWN, OUT) for y in range(Y)
-        ]
+        grads = (grads0, grads1)[half]
+        wide = [grads[:, y, step * OWN:(step + 1) * OWN, :].reshape(LINE * OWN, OUT) for y in range(Y)]
         return jnp.transpose(jnp.concatenate(wide, axis=0).astype(jnp.float32))
 
     grad0 = [gradient(0, half) for half in range(2)]
@@ -416,9 +411,11 @@
     for half in range(2):
         direction = grad0[half] / shift_rho + split_nt(scaled0, factor(0, half))
         moves.append((-MOVE * direction).astype(jnp.bfloat16))
-    for load in loads[2 * Y:]:
+    for load in loads[2 * Y:4 * Y]:
         load.wait()
     projected = project(grad1, 1)
+    for load in loads[4 * Y:]:
+        load.wait()
     _, aux1, blend1 = blends(result[1], result[0])
     result[0] = blend1
     result[1] = beta_coef * aux1 + (1.0 - beta_coef) * blend1
@@ -468,7 +465,7 @@
     return pl.pallas_call(
         finish_kernel,
         out_shape=(pltpu.HBM((ROWS, OUT), jnp.float32),) * 2,
-        in_specs=[pl.BlockSpec(memory_space=pltpu.SMEM)] + [vmem] * 4 + [far] * 4,
+        in_specs=[pl.BlockSpec(memory_space=pltpu.SMEM)] + [vmem] * 5 + [far] * 4,
         out_specs=(far, far),
         scratch_shapes=[
             pltpu.VMEM((2, ROWS, OUT), jnp.float32),
@@ -480,7 +477,7 @@
         ],
         compiler_params=pltpu.CompilerParams(vmem_limit_bytes=32 * MIB),
         name="finish",
-    )(indices, grads, own_grad, own_cross, spectrum, factors, weights, primary, auxiliary)
+    )(indices, *grads, own_grad, own_cross, spectrum, factors, weights, primary, auxiliary)
 
 
 def on_device(features, targets, primary, auxiliary, factors, spectrum, indices):
@@ -527,7 +524,9 @@
     own_grad, tosend = collect(received, extra)
     factors = factors.reshape(STEPS, LINE, Y, 2, OWN, D)
     weights, own_cross = cross(indices, block, other_block, idx_halves, factors, own_grad)
-    grads = lax.all_to_all(tosend, ALL, 0, 0, tiled=True).reshape(LINE, Y, 2, STEPS * OWN, OUT)
+    grads = lax.all_to_all(tosend, ("row", "y"), 0, 0, tiled=True).reshape(LINE, Y, STEPS * OWN, OUT)
+    grads, weights = lax.optimization_barrier((grads, weights))
+    grads = (grads, swap(grads))
     return finish(indices, grads, own_grad, own_cross, spectrum, factors, weights, primary, auxiliary)
 
 

time: 113 us -> 111 us (0.982)
  waiting for transfers between devices: 18.3 us -> 16.5 us
  starting transfers between devices: 23.5 us -> 24.8 us
  Pallas kernels: 49.6 us -> 48.4 us
    all_to_all x1, waiting for transfers between devices: 3.63 us -> 0.01 us  [on_device(): lax.all_to_all(tosend, ('row', 'y'), 0, 0, tiled=True)]
    ppermute x4 -> x5, waiting for transfers between devices: 0.01 us -> 1.55 us  [on_device(): swap = lambda x: lax.ppermute(x, 'core', [(0, 1), (1, 0)])]
    ppermute x4 -> x5, starting transfers between devices: 7.55 us -> 8.53 us  [on_device(): swap = lambda x: lax.ppermute(x, 'core', [(0, 1), (1, 0)])]
  transfers between devices with their start and end apart: 13 -> 14, of which waited for: 3 -> 3; matrix products, arithmetic and copies ran while one was open for 0% -> 0% of each run, Pallas kernels for 34% -> 34%
where the time goes in v4:
time: 111 us
  Pallas kernels  48.4 us (44%)
  starting transfers between devices  24.8 us (22%)
  blocking collectives  18.7 us (17%)
  waiting for transfers between devices  16.5 us (15%)
    pallas_call x4, Pallas kernels, products(): pl.pallas_call(functools.partial(product_kernel, pieces=len(pieces), sums...  19.2 us
    all_to_all x1, blocking collectives, on_device(): exchange = lambda x: lax.all_to_all(x, 'row', 0, 0, tiled=True)  18.7 us
    pallas_call x1, Pallas kernels, cross(): pl.pallas_call(cross_kernel, grid=(2, tiles), out_shape=(pltpu.HBM((ROWS,...  14.6 us
    ppermute x5, starting transfers between devices, on_device(): swap = lambda x: lax.ppermute(x, 'core', [(0, 1), (1, 0)])  8.53 us
    ppermute x7, starting transfers between devices, shift(): return lax.ppermute(x, 'y', [(y, (y + by) % Y) for y in range(Y)])  8.1 us
    ppermute x7, waiting for transfers between devices, shift(): return lax.ppermute(x, 'y', [(y, (y + by) % Y) for y in range(Y)])  7.78 us
    pallas_call x1, Pallas kernels, finish(): pl.pallas_call(finish_kernel, out_shape=(pltpu.HBM((ROWS, OUT), jnp.float...  7.66 us
    all_to_all x1, waiting for transfers between devices, on_device(): exchange = lambda x: lax.all_to_all(x, 'row', 0, 0, tiled=True)  7.12 us
  transfers between devices with their start and end apart: 14, of which 3 were waited for; matrix products, arithmetic and copies ran while one was open for 0% of the time, Pallas kernels for 34%

profile of v4, /device:TPU:1, one launch (start us, length us, event | category | flops | bytes accessed | tf_op | source)
XLA Modules:
  0.0 110.6 jit_solution(17254754032006996045)
XLA Ops:
  0.6 0.0 copy-start.1
  0.7 0.0 copy-start
  0.7 0.0 copy-start.3
  0.7 3.4 %pick.1 = bf16[16,32,512]{2,1,0:T(8,128)(2,1)} custom-call(s32[2,2048]{1,0:T(2,128)} %idx.7, bf16[2048,512]{1,0:T(8,128)(2,1)} %refs_1_.5), custom_call_target="tpu_custom_call" | custom-call | tf_op jit(solution)/shard_map/pick/pallas_call | solution.py:93
  4.1 1.5 %collective-permute-start.6 = (bf16[2048,512]{1,0:T(8,128)(2,1)}, bf16[2048,512]{1,0:T(8,128)(2,1)S(1)}, u32[]{:S(2)}, u32[]{:S(2)}) collective-permute-start(bf16[2048,512]{1,0:T(8,128)(2,1)} %refs_1_.5), channel_id=1, source_target_pairs={{0,1},{1,0},{2,3},{3,2},{4,5},{5,4},{6,7},{7,6},{8,9},{9,8},{10,11... | collective-permute-start | bytes 6291464 | tf_op jit(solution)/shard_map/ppermute | solution.py:485
  5.6 0.0 copy-done
  5.6 0.1 collective-permute-start.2
  5.7 0.4 collective-permute-start.3
  6.1 18.7 %all_to_all.15.refs_0_.refs_8_ = bf16[16,32,512]{2,1,0:T(8,128)(2,1)S(1)} all-to-all(bf16[16,32,512]{2,1,0:T(8,128)(2,1)} %pick.1), channel_id=1, replica_groups=mesh['row'=16,'y'=4,'core'=2] {'row'}, dimensions={0} | all-to-all | bytes 1048576 | tf_op jit(solution)/shard_map/all_to_all | solution.py:486
  24.8 1.3 %collective-permute-start = (bf16[16,32,512]{2,1,0:T(8,128)(2,1)S(1)}, bf16[16,32,512]{2,1,0:T(8,128)(2,1)S(1)}, u32[]{:S(2)}, u32[]{:S(2)}) collective-permute-start(bf16[16,32,512]{2,1,0:T(8,128)(2,1)S(1)} %all_to_all.15.refs_0_.refs_8_), channel_id=1, source_target_pairs={{0,2},{2,4},{4,6},{6,0},{1,3},{3,5},{5,7},{7,1},{8,10},{10,12},{12... | collective-permute-start | bytes 1572872 | tf_op jit(solution)/shard_map/ppermute | solution.py:489
  26.1 1.4 %collective-permute-start.1 = (bf16[16,32,512]{2,1,0:T(8,128)(2,1)S(1)}, bf16[16,32,512]{2,1,0:T(8,128)(2,1)S(1)}, u32[]{:S(2)}, u32[]{:S(2)}) collective-permute-start(bf16[16,32,512]{2,1,0:T(8,128)(2,1)S(1)} %all_to_all.15.refs_0_.refs_8_), channel_id=1, source_target_pairs={{0,6},{2,0},{4,2},{6,4},{1,7},{3,1},{5,3},{7,5},{8,14},{10,8},{12,... | collective-permute-start | bytes 1572872 | tf_op jit(solution)/shard_map/ppermute | solution.py:489
  27.5 0.0 collective-permute-done.2.other_pri
  27.5 0.0 collective-permute-done.3.other_aux
  27.6 2.7 %prepare.1 = (bf16[2048,256]{1,0:T(8,128)(2,1)S(1)}, bf16[2048,256]{1,0:T(8,128)(2,1)S(1)}, f32[32,128]{1,0:T(8,128)S(1)}) custom-call(s32[2,2048]{1,0:T(2,128)S(1)} %copy-done.4, bf16[2048,128]{1,0:T(8,128)(2,1)S(1)} %copy-done.3, f32[2048,128]{1,0:T(8,128)S(1)} %copy-done, f32[2048,128]{1,0:T(8,128)S(1)} %copy-done.1, ...), custom_call_target="tpu_custom_call" | custom-call | tf_op jit(solution)/shard_map/prepare/pallas_call | solution.py:128
  30.3 7.8 %collective-permute-done.refs_0_.refs_9_ = bf16[16,32,512]{2,1,0:T(8,128)(2,1)S(1)} collective-permute-done((bf16[16,32,512]{2,1,0:T(8,128)(2,1)S(1)}, bf16[16,32,512]{2,1,0:T(8,128)(2,1)S(1)}, u32[]{:S(2)}, u32[]{:S(2)}) %collective-permute-start) | collective-permute-done | bytes 524320 | tf_op jit(solution)/shard_map/ppermute | solution.py:489
  38.1 0.0 collective-permute-done.1.refs_0_.refs_10_
  38.1 1.0 collective-permute-start.4
  39.2 1.8 %collective-permute-start.5 = (bf16[8,32,512]{2,1,0:T(8,128)(2,1)S(1)}, bf16[8,32,512]{2,1,0:T(8,128)(2,1)S(1)}, u32[]{:S(2)}, u32[]{:S(2)}) collective-permute-start(bf16[8,32,512]{2,1,0:T(8,128)(2,1)S(1)} %slice.7), channel_id=1, source_target_pairs={{0,6},{2,0},{4,2},{6,4},{1,7},{3,1},{5,3},{7,5},{8,14},{10,8},{12,... | collective-permute-start | bytes 786440 | tf_op jit(solution)/shard_map/ppermute | solution.py:489
  40.9 0.0 collective-permute-done.6.refs_2_.refs_3_
  40.9 4.9 %products.4 = (bf16[16,32,128]{2,1,0:T(8,128)(2,1)}, f32[2,2048]{1,0:T(2,128)S(1)}) custom-call(bf16[16,32,512]{2,1,0:T(8,128)(2,1)S(1)} %collective-permute-done.refs_0_.refs_9_, bf16[2048,512]{1,0:T(8,128)(2,1)S(1)} %copy-done.2, bf16[2048,512]{1,0:T(8,128)(2,1)S(1)} %collective-permute-done.6.refs_2_.refs_3_, ...), custom_call_target="tpu_custom_call" | custom-call | flops 3221225472 | bytes 1048576 | tf_op jit(solution)/shard_map/products/pallas_call | solution.py:219
  45.8 1.2 %collective-permute-start.7 = (bf16[16,32,128]{2,1,0:T(8,128)(2,1)}, bf16[16,32,128]{2,1,0:T(8,128)(2,1)S(1)}, u32[]{:S(2)}, u32[]{:S(2)}) collective-permute-start(bf16[16,32,128]{2,1,0:T(8,128)(2,1)} %get-tuple-element.47), channel_id=1, source_target_pairs={{0,6},{2,0},{4,2},{6,4},{1,7},{3,1},{5,3},{7,5},{8,14},{10,8},{12,... | collective-permute-start | bytes 393224 | tf_op jit(solution)/shard_map/ppermute | solution.py:489
  47.0 4.3 %products.5 = bf16[16,32,128]{2,1,0:T(8,128)(2,1)} custom-call(bf16[16,32,512]{2,1,0:T(8,128)(2,1)S(1)} %collective-permute-done.1.refs_0_.refs_10_, bf16[2048,512]{1,0:T(8,128)(2,1)S(1)} %copy-done.2, bf16[2048,512]{1,0:T(8,128)(2,1)S(1)} %collective-permute-done.6.refs_2_.refs_3_, bf16[2048,256]{1,0:T(8,128)(2,1)S(1)} %get-tuple-element.45.refs_3_.refs_4_, ...), custom_call_target="tpu_custom_call" | custom-call | flops 3221225472 | bytes 1048576 | tf_op jit(solution)/shard_map/products/pallas_call | solution.py:219
  51.3 0.3 collective-permute-start.8
  51.6 0.0 collective-permute-done.4.refs_0_.refs_11_
  51.6 0.0 collective-permute-done.5.refs_1_.refs_12_
  51.6 4.3 %products.6 = bf16[16,32,128]{2,1,0:T(8,128)(2,1)} custom-call(bf16[8,32,512]{2,1,0:T(8,128)(2,1)S(1)} %collective-permute-done.4.refs_0_.refs_11_, bf16[8,32,512]{2,1,0:T(8,128)(2,1)S(1)} %collective-permute-done.5.refs_1_.refs_12_, bf16[2048,512]{1,0:T(8,128)(2,1)S(1)} %copy-done.2, bf16[2048,512]{1,0:T(8,128)(2,1)S(1)} %collective-permute-done.6.refs_2_.refs_3_, ...), custom_call_target="tpu_custom_call" | custom-call | flops 3221225472 | bytes 1048576 | tf_op jit(solution)/shard_map/products/pallas_call | solution.py:219
  56.0 1.1 collective-permute-start.9
  57.1 0.0 collective-permute-done.8.refs_7_
  57.1 0.0 collective-permute-done.7.refs_6_
  57.1 5.6 %products.7 = (f32[16,32,128]{2,1,0:T(8,128)S(1)}, bf16[4,16,32,512]{3,2,1,0:T(8,128)(2,1)}) custom-call(bf16[16,32,512]{2,1,0:T(8,128)(2,1)S(1)} %all_to_all.15.refs_0_.refs_8_, bf16[2048,512]{1,0:T(8,128)(2,1)S(1)} %copy-done.2, bf16[2048,512]{1,0:T(8,128)(2,1)S(1)} %collective-permute-done.6.refs_2_.refs_3_, ...), custom_call_target="tpu_custom_call" | custom-call | flops 3221225472 | bytes 1048576 | tf_op jit(solution)/shard_map/products/pallas_call | solution.py:219
  62.7 0.0 collective-permute-done.9
  62.7 0.7 add_convert_fusion
  63.4 5.5 %collective-permute-start.10 = (bf16[64,2,16,512]{3,2,1,0:T(8,128)(2,1)}, bf16[64,2,16,512]{3,2,1,0:T(8,128)(2,1)}, u32[]{:S(2)}, u32[]{:S(2)}) collective-permute-start(bf16[64,2,16,512]{3,2,1,0:T(8,128)(2,1)} %bitcast.15), channel_id=1, source_target_pairs={{0,1},{1,0},{2,3},{3,2},{4,5},{5,4},{6,7},{7,6},{8,9},{9,8},{10,11... | collective-permute-start | bytes 6291464 | tf_op jit(solution)/shard_map/ppermute | solution.py:485
  68.9 0.2 convert_element_type.15
  69.1 0.1 constant_dynamic-slice_fusion.1
  69.3 3.5 %all-to-all-start.1 = ((bf16[16,32,128]{2,1,0:T(8,128)(2,1)}), bf16[16,32,128]{2,1,0:T(8,128)(2,1)S(1)}, u32[]{:S(2)}, u32[]{:S(2)}) async-start(bf16[16,32,128]{2,1,0:T(8,128)(2,1)} %add_convert_fusion), calls=%async_computation.1 | async-start | bytes 262144 | tf_op jit(solution)/shard_map/all_to_all | solution.py:486
  72.8 0.1 reshape.21.idx_ref
  72.9 7.1 %all-to-all-done.1.received = bf16[16,32,128]{2,1,0:T(8,128)(2,1)S(1)} async-done(((bf16[16,32,128]{2,1,0:T(8,128)(2,1)}), bf16[16,32,128]{2,1,0:T(8,128)(2,1)S(1)}, u32[]{:S(2)}, u32[]{:S(2)}) %all-to-all-start.1) | async-done | bytes 131104 | tf_op jit(solution)/shard_map/all_to_all | solution.py:486
  80.1 0.8 collect.1
  80.9 4.6 %all-to-all-start.2 = ((bf16[64,32,128]{2,1,0:T(8,128)(2,1)}), bf16[64,32,128]{2,1,0:T(8,128)(2,1)S(1)}, u32[]{:S(2)}, u32[]{:S(2)}) async-start(bf16[64,32,128]{2,1,0:T(8,128)(2,1)} %get-tuple-element.57), calls=%async_computation.2 | async-start | bytes 1048576 | tf_op jit(solution)/shard_map/all_to_all | solution.py:527
  85.6 0.0 collective-permute-done.10.other0.other1
  85.6 0.0 copy-start.5
  85.6 14.6 %cross.1 = (bf16[2048,512]{1,0:T(8,128)(2,1)}, bf16[16,2048]{1,0:T(8,128)(2,1)S(1)}) custom-call(s32[2,2048]{1,0:T(2,128)S(1)} %copy-done.4, f32[2,2,2,512]{3,2,1,0:T(2,128)S(1)} %reshape.21.idx_ref, bf16[64,2,16,512]{3,2,1,0:T(8,128)(2,1)} %bitcast.16, bf16[64,2,16,512]{3,2,1,0:T(8,128)(2,1)} %collective-permute-done.10.other0.other1, ...), custom_call_target="tpu_custom_call" | custom-call | flops 8589934592 | bytes 8388608 | tf_op jit(solution)/shard_map/cross/pallas_call | solution.py:305
  100.2 0.0 all-to-all-done.2
  100.2 1.0 collective-permute-start.11
  101.2 1.5 %collective-permute-done.11.grads1 = bf16[16,4,32,128]{3,2,1,0:T(8,128)(2,1)S(1)} collective-permute-done((bf16[16,4,32,128]{3,2,1,0:T(8,128)(2,1)S(1)}, bf16[16,4,32,128]{3,2,1,0:T(8,128)(2,1)S(1)}, u32[]{:S(2)}, u32[]{:S(2)}) %collective-permute-start.11) | collective-permute-done | bytes 524320 | tf_op jit(solution)/shard_map/ppermute | solution.py:485
  102.7 0.0 copy-done.5
  102.7 7.7 %finish.1 = (f32[2048,128]{1,0:T(8,128)}, f32[2048,128]{1,0:T(8,128)}) custom-call(s32[2,2048]{1,0:T(2,128)S(1)} %copy-done.4, bf16[16,4,32,128]{3,2,1,0:T(8,128)(2,1)S(1)} %bitcast.12, bf16[16,4,32,128]{3,2,1,0:T(8,128)(2,1)S(1)} %collective-permute-done.11.grads1, f32[32,128]{1,0:T(8,128)S(1)} %get-tuple-element.59.after.own_grad, ...), custom_call_target="tpu_custom_call" | custom-call | tf_op jit(solution)/shard_map/finish/pallas_call | solution.py:465
  (11 shorter events, 0.1 us)
Async XLA Ops:
  0.6 26.9 %copy-start.4 = (s32[2,2048]{1,0:T(2,128)S(1)}, s32[2,2048]{1,0:T(2,128)}, u32[]{:S(2)}) copy-start(s32[2,2048]{1,0:T(2,128)} %idx.7) | copy-start | bytes 49156
  0.6 5.0 %copy-start.1 = (f32[2048,128]{1,0:T(8,128)S(1)}, f32[2048,128]{1,0:T(8,128)}, u32[]{:S(2)}) copy-start(f32[2048,128]{1,0:T(8,128)} %aux.2) | copy-start | bytes 3145732
  0.7 4.9 %copy-start = (f32[2048,128]{1,0:T(8,128)S(1)}, f32[2048,128]{1,0:T(8,128)}, u32[]{:S(2)}) copy-start(f32[2048,128]{1,0:T(8,128)} %pri.2) | copy-start | bytes 3145732
  0.7 26.9 %copy-start.3 = (bf16[2048,128]{1,0:T(8,128)(2,1)S(1)}, bf16[2048,128]{1,0:T(8,128)(2,1)}, u32[]{:S(2)}) copy-start(bf16[2048,128]{1,0:T(8,128)(2,1)} %tgt.1) | copy-start | bytes 1572868
  4.1 36.8 %collective-permute-start.6 = (bf16[2048,512]{1,0:T(8,128)(2,1)}, bf16[2048,512]{1,0:T(8,128)(2,1)S(1)}, u32[]{:S(2)}, u32[]{:S(2)}) collective-permute-start(bf16[2048,512]{1,0:T(8,128)(2,1)} %refs_1_.5), channel_id=1, source_target_pairs={{0,1},{1,0},{2,3},{3,2},{4,5},{5,4},{6,7},{7,6},{8,9},{9,8},{10,11... | collective-permute-start | bytes 6291464 | tf_op jit(solution)/shard_map/ppermute | solution.py:485
  5.6 22.0 %collective-permute-start.2 = (f32[2048,128]{1,0:T(8,128)S(1)}, f32[2048,128]{1,0:T(8,128)S(1)}, u32[]{:S(2)}, u32[]{:S(2)}) collective-permute-start(f32[2048,128]{1,0:T(8,128)S(1)} %copy-done), channel_id=1, source_target_pairs={{0,1},{1,0},{2,3},{3,2},{4,5},{5,4},{6,7},{7,6},{8,9},{9,8},{10,11... | collective-permute-start | bytes 3145736 | tf_op jit(solution)/shard_map/ppermute | solution.py:485
  5.7 21.9 %collective-permute-start.3 = (f32[2048,128]{1,0:T(8,128)S(1)}, f32[2048,128]{1,0:T(8,128)S(1)}, u32[]{:S(2)}, u32[]{:S(2)}) collective-permute-start(f32[2048,128]{1,0:T(8,128)S(1)} %copy-done.1), channel_id=1, source_target_pairs={{0,1},{1,0},{2,3},{3,2},{4,5},{5,4},{6,7},{7,6},{8,9},{9,8},{10,11... | collective-permute-start | bytes 3145736 | tf_op jit(solution)/shard_map/ppermute | solution.py:485
  24.8 16.1 %copy-start.2 = (bf16[2048,512]{1,0:T(8,128)(2,1)S(1)}, bf16[2048,512]{1,0:T(8,128)(2,1)}, u32[]{:S(2)}) copy-start(bf16[2048,512]{1,0:T(8,128)(2,1)} %refs_1_.5) | copy-start | bytes 6291460
  24.8 13.3 %collective-permute-start = (bf16[16,32,512]{2,1,0:T(8,128)(2,1)S(1)}, bf16[16,32,512]{2,1,0:T(8,128)(2,1)S(1)}, u32[]{:S(2)}, u32[]{:S(2)}) collective-permute-start(bf16[16,32,512]{2,1,0:T(8,128)(2,1)S(1)} %all_to_all.15.refs_0_.refs_8_), channel_id=1, source_target_pairs={{0,2},{2,4},{4,6},{6,0},{1,3},{3,5},{5,7},{7,1},{8,10},{10,12},{12... | collective-permute-start | bytes 1572872 | tf_op jit(solution)/shard_map/ppermute | solution.py:489
  26.1 12.0 %collective-permute-start.1 = (bf16[16,32,512]{2,1,0:T(8,128)(2,1)S(1)}, bf16[16,32,512]{2,1,0:T(8,128)(2,1)S(1)}, u32[]{:S(2)}, u32[]{:S(2)}) collective-permute-start(bf16[16,32,512]{2,1,0:T(8,128)(2,1)S(1)} %all_to_all.15.refs_0_.refs_8_), channel_id=1, source_target_pairs={{0,6},{2,0},{4,2},{6,4},{1,7},{3,1},{5,3},{7,5},{8,14},{10,8},{12,... | collective-permute-start | bytes 1572872 | tf_op jit(solution)/shard_map/ppermute | solution.py:489
  38.1 13.6 %collective-permute-start.4 = (bf16[8,32,512]{2,1,0:T(8,128)(2,1)S(1)}, bf16[8,32,512]{2,1,0:T(8,128)(2,1)S(1)}, u32[]{:S(2)}, u32[]{:S(2)}) collective-permute-start(bf16[8,32,512]{2,1,0:T(8,128)(2,1)S(1)} %slice.6), channel_id=1, source_target_pairs={{0,2},{2,4},{4,6},{6,0},{1,3},{3,5},{5,7},{7,1},{8,10},{10,12},{12... | collective-permute-start | bytes 786440 | tf_op jit(solution)/shard_map/ppermute | solution.py:489
  39.2 12.5 %collective-permute-start.5 = (bf16[8,32,512]{2,1,0:T(8,128)(2,1)S(1)}, bf16[8,32,512]{2,1,0:T(8,128)(2,1)S(1)}, u32[]{:S(2)}, u32[]{:S(2)}) collective-permute-start(bf16[8,32,512]{2,1,0:T(8,128)(2,1)S(1)} %slice.7), channel_id=1, source_target_pairs={{0,6},{2,0},{4,2},{6,4},{1,7},{3,1},{5,3},{7,5},{8,14},{10,8},{12,... | collective-permute-start | bytes 786440 | tf_op jit(solution)/shard_map/ppermute | solution.py:489
  45.8 11.3 %collective-permute-start.7 = (bf16[16,32,128]{2,1,0:T(8,128)(2,1)}, bf16[16,32,128]{2,1,0:T(8,128)(2,1)S(1)}, u32[]{:S(2)}, u32[]{:S(2)}) collective-permute-start(bf16[16,32,128]{2,1,0:T(8,128)(2,1)} %get-tuple-element.47), channel_id=1, source_target_pairs={{0,6},{2,0},{4,2},{6,4},{1,7},{3,1},{5,3},{7,5},{8,14},{10,8},{12,... | collective-permute-start | bytes 393224 | tf_op jit(solution)/shard_map/ppermute | solution.py:489
  51.3 5.7 %collective-permute-start.8 = (bf16[16,32,128]{2,1,0:T(8,128)(2,1)}, bf16[16,32,128]{2,1,0:T(8,128)(2,1)S(1)}, u32[]{:S(2)}, u32[]{:S(2)}) collective-permute-start(bf16[16,32,128]{2,1,0:T(8,128)(2,1)} %products.5), channel_id=1, source_target_pairs={{0,2},{2,4},{4,6},{6,0},{1,3},{3,5},{5,7},{7,1},{8,10},{10,12},{12... | collective-permute-start | bytes 393224 | tf_op jit(solution)/shard_map/ppermute | solution.py:489
  56.0 6.7 %collective-permute-start.9 = (bf16[16,32,128]{2,1,0:T(8,128)(2,1)}, bf16[16,32,128]{2,1,0:T(8,128)(2,1)S(1)}, u32[]{:S(2)}, u32[]{:S(2)}) collective-permute-start(bf16[16,32,128]{2,1,0:T(8,128)(2,1)} %products.6), channel_id=1, source_target_pairs={{0,4},{2,6},{4,0},{6,2},{1,5},{3,7},{5,1},{7,3},{8,12},{10,14},{12... | collective-permute-start | bytes 393224 | tf_op jit(solution)/shard_map/ppermute | solution.py:489
  63.4 22.2 %collective-permute-start.10 = (bf16[64,2,16,512]{3,2,1,0:T(8,128)(2,1)}, bf16[64,2,16,512]{3,2,1,0:T(8,128)(2,1)}, u32[]{:S(2)}, u32[]{:S(2)}) collective-permute-start(bf16[64,2,16,512]{3,2,1,0:T(8,128)(2,1)} %bitcast.15), channel_id=1, source_target_pairs={{0,1},{1,0},{2,3},{3,2},{4,5},{5,4},{6,7},{7,6},{8,9},{9,8},{10,11... | collective-permute-start | bytes 6291464 | tf_op jit(solution)/shard_map/ppermute | solution.py:485
  69.3 10.8 %all-to-all-start.1 = ((bf16[16,32,128]{2,1,0:T(8,128)(2,1)}), bf16[16,32,128]{2,1,0:T(8,128)(2,1)S(1)}, u32[]{:S(2)}, u32[]{:S(2)}) async-start(bf16[16,32,128]{2,1,0:T(8,128)(2,1)} %add_convert_fusion), calls=%async_computation.1 | async-start | bytes 262144 | tf_op jit(solution)/shard_map/all_to_all | solution.py:486
  80.9 19.3 %all-to-all-start.2 = ((bf16[64,32,128]{2,1,0:T(8,128)(2,1)}), bf16[64,32,128]{2,1,0:T(8,128)(2,1)S(1)}, u32[]{:S(2)}, u32[]{:S(2)}) async-start(bf16[64,32,128]{2,1,0:T(8,128)(2,1)} %get-tuple-element.57), calls=%async_computation.2 | async-start | bytes 1048576 | tf_op jit(solution)/shard_map/all_to_all | solution.py:527
  85.6 17.2 %copy-start.5 = (f32[2,512]{1,0:T(2,128)S(1)}, f32[2,512]{1,0:T(2,128)}, u32[]{:S(2)}) copy-start(f32[2,512]{1,0:T(2,128)} %spectrum.1) | copy-start | bytes 12292
  100.2 2.5 %collective-permute-start.11 = (bf16[16,4,32,128]{3,2,1,0:T(8,128)(2,1)S(1)}, bf16[16,4,32,128]{3,2,1,0:T(8,128)(2,1)S(1)}, u32[]{:S(2)}, u32[]{:S(2)}) collective-permute-start(bf16[16,4,32,128]{3,2,1,0:T(8,128)(2,1)S(1)} %bitcast.11), channel_id=1, source_target_pairs={{0,1},{1,0},{2,3},{3,2},{4,5},{5,4},{6,7},{7,6},{8,9},{9,8},{10,11... | collective-permute-start | bytes 1572872 | tf_op jit(solution)/shard_map/ppermute | solution.py:485
